TPU v7x, 32 devices: a whole 2x2x4 slice. The times are simulated.
32 devices in a mesh: dp: 1, mp: 32 (over z, y, x, core).
Axes of the slice: x: 2, y: 2, z: 4, core: 2. Of those that a mesh axis runs over, the one named last changes fastest.
Arguments:
- layer_input: bfloat16 [1, 32, 16, 128, 128], P('dp', 'mp'), may hold values from -6 to 6
- cotangent: bfloat16 [1, 32, 16, 128, 128], P('dp', 'mp'), may hold values from -6 to 6
- spec_weight: bfloat16 [16, 16, 16, 2, 1024], P(None, None, None, None, 'mp'), may hold values from -1 to 1
- point_weight: bfloat16 [16, 16], replicated, may hold values from -1.5 to 1.5
- bias_term: float32 [16], replicated, may hold values from -3 to 3
Outputs:
- input_grad: bfloat16 [1, 32, 16, 128, 128], P('dp', 'mp')
- spec_grad: float32 [16, 16, 16, 2, 1024], P(None, None, None, None, 'mp')
- point_grad: float32 [16, 16], replicated
- bias_grad: float32 [16], replicated
All inputs are finite; a program needn't handle non-finite values.
Results may differ from a plain program's by a relative error of at most 0.017.
Values may be sent and summed in bfloat16 or wider, within the bound.
A program may use at most 64 MiB of HBM per device.

v0:
```python
import math

import jax
import jax.numpy as jnp
from jax import lax
from jax.sharding import PartitionSpec as P

SQRT_TWO_PI = math.sqrt(2.0 / math.pi)


def mixed_dot(formula, first_op, second_op):
    return jnp.einsum(formula, first_op, second_op, preferred_element_type=jnp.float32)


def dft_table(length, freq_count, signed):
    frequency = jnp.arange(freq_count, dtype=jnp.int32)
    if signed:
        frequency = jnp.where(frequency >= freq_count // 2, frequency - freq_count, frequency)
    places = jnp.arange(length, dtype=jnp.int32)
    phases = jnp.mod(places[:, None] * frequency[None, :], length).astype(jnp.float32) * (
        2.0 * math.pi / length
    )
    return jnp.concatenate([jnp.cos(phases), -jnp.sin(phases)], axis=1).astype(jnp.bfloat16)


def to_spectrum(values, table_x, table_y, table_z, factor):
    samples, local_z, channels = (values.shape[0], values.shape[1], values.shape[2])
    half_x = table_x.shape[1] // 2
    half_y = table_y.shape[1] // 2
    half_z = table_z.shape[1] // 2
    along_y = mixed_dot("nzcxy,yk->nzcxk", values, table_y).astype(jnp.bfloat16)
    partial_value = mixed_dot("nzcxk,xa->nzcak", along_y, table_x)
    real_part = partial_value[..., :half_x, :half_y] - partial_value[..., half_x:, half_y:]
    imag_part = partial_value[..., :half_x, half_y:] + partial_value[..., half_x:, :half_y]
    planes = (
        jnp.stack([real_part, imag_part], axis=3)
        .reshape(samples, local_z, channels, 2, half_x * half_y)
        .astype(jnp.bfloat16)
    )
    whole_z = mixed_dot(
        "nzcrp,zk->nkcrp",
        lax.all_to_all(planes, "mp", split_axis=4, concat_axis=1, tiled=True),
        table_z,
    )
    real_z = whole_z[:, :half_z, :, 0] - whole_z[:, half_z:, :, 1]
    imag_z = whole_z[:, :half_z, :, 1] + whole_z[:, half_z:, :, 0]
    return (factor * jnp.stack([real_z, imag_z], axis=3)).astype(jnp.bfloat16)


def to_field(spectrum, table_x, table_y, table_z, factor):
    depth_z = table_z.shape[0]
    half_z = table_z.shape[1] // 2
    cells_x = table_x.shape[0]
    half_x = table_x.shape[1] // 2
    half_y = table_y.shape[1] // 2
    waves_z = table_z.reshape(depth_z, 2, half_z)
    whole_z = mixed_dot("nkcrp,zqk->nzqcrp", spectrum, waves_z)
    real_z = whole_z[:, :, 0, :, 0] + whole_z[:, :, 1, :, 1]
    imag_z = whole_z[:, :, 0, :, 1] - whole_z[:, :, 1, :, 0]
    pencil_data = jnp.stack([real_z, imag_z], axis=3).astype(jnp.bfloat16)
    waves_x = table_x.reshape(cells_x, 2, half_x)
    pencil_rows = lax.all_to_all(pencil_data, "mp", split_axis=1, concat_axis=4, tiled=True)
    samples = pencil_rows.shape[0]
    local_z = pencil_rows.shape[1]
    channels = pencil_rows.shape[2]
    mode_grid = pencil_rows.reshape(samples, local_z, channels, 2, half_x, half_y)
    along_x = mixed_dot("nzcrab,xqa->nzcxqrb", mode_grid, waves_x)
    real_x = along_x[:, :, :, :, 0, 0] + along_x[:, :, :, :, 1, 1]
    imag_x = along_x[:, :, :, :, 0, 1] - along_x[:, :, :, :, 1, 0]
    half_spec = jnp.concatenate([real_x, imag_x], axis=-1).astype(jnp.bfloat16)
    return factor * mixed_dot("nzcxk,yk->nzcxy", half_spec, table_y)


def mix_modes(spectrum, weight, mode_scale):
    formula = "nkip,kiop->nkop"
    spec_re, spec_im = (spectrum[:, :, :, 0], spectrum[:, :, :, 1])
    weight_re, weight_im = (weight[:, :, :, 0], weight[:, :, :, 1])
    real_part = mixed_dot(formula, spec_re, weight_re) - mixed_dot(formula, spec_im, weight_im)
    imag_part = mixed_dot(formula, spec_re, weight_im) + mixed_dot(formula, spec_im, weight_re)
    return (
        mode_scale[None, :, None, None, None] * jnp.stack([real_part, imag_part], axis=3)
    ).astype(jnp.bfloat16)


def back_modes(grads, weight, mode_scale):
    formula = "nkop,kiop->nkip"
    grad_re, grad_im = (grads[:, :, :, 0], grads[:, :, :, 1])
    weight_re, weight_im = (weight[:, :, :, 0], weight[:, :, :, 1])
    real_part = mixed_dot(formula, grad_re, weight_re) + mixed_dot(formula, grad_im, weight_im)
    imag_part = mixed_dot(formula, grad_im, weight_re) - mixed_dot(formula, grad_re, weight_im)
    return (
        mode_scale[None, :, None, None, None] * jnp.stack([real_part, imag_part], axis=3)
    ).astype(jnp.bfloat16)


def weight_terms(spectra, grads, mode_scale):
    formula = "nkip,nkop->kiop"
    spec_re, spec_im = (spectra[:, :, :, 0], spectra[:, :, :, 1])
    grad_re, grad_im = (grads[:, :, :, 0], grads[:, :, :, 1])
    real_part = mixed_dot(formula, spec_re, grad_re) + mixed_dot(formula, spec_im, grad_im)
    imag_part = mixed_dot(formula, spec_re, grad_im) - mixed_dot(formula, spec_im, grad_re)
    return mode_scale[:, None, None, None, None] * jnp.stack([real_part, imag_part], axis=3)


def gelu_slope(pre_act):
    inner_arg = SQRT_TWO_PI * (pre_act + 0.044715 * pre_act * pre_act * pre_act)
    tanh_val = jnp.tanh(inner_arg)
    return 0.5 * (1.0 + tanh_val) + 0.5 * pre_act * (1.0 - tanh_val * tanh_val) * SQRT_TWO_PI * (
        1.0 + 0.134145 * pre_act * pre_act
    )


def shards(layer_input, cotangent, spec_weight, point_weight, bias_term):
    local_z, cells_x, cells_y = (layer_input.shape[1], layer_input.shape[3], layer_input.shape[4])
    depth_z = local_z * lax.axis_size("mp")
    mode_count = spec_weight.shape[0]
    table_x = dft_table(cells_x, 2 * mode_count, True)
    table_y = dft_table(cells_y, 2 * mode_count, True)
    table_z = dft_table(depth_z, mode_count, False)
    factor = 1.0 / math.sqrt(cells_x * cells_y * depth_z)
    mode_scale = jnp.where(jnp.arange(mode_count) == 0, 1.0, 2.0).astype(jnp.float32)
    spectrum = to_spectrum(layer_input, table_x, table_y, table_z, factor)
    mixed_spec = mix_modes(spectrum, spec_weight, mode_scale)
    spectral = to_field(mixed_spec, table_x, table_y, table_z, factor)
    pre_act = (
        spectral
        + mixed_dot("nzixy,io->nzoxy", layer_input, point_weight)
        + bias_term[None, None, :, None, None]
    )
    grad_pre = (cotangent.astype(jnp.float32) * gelu_slope(pre_act)).astype(jnp.bfloat16)
    grad_spectrum = to_spectrum(grad_pre, table_x, table_y, table_z, factor)
    back_spec = back_modes(grad_spectrum, spec_weight, mode_scale)
    input_grad = (
        to_field(back_spec, table_x, table_y, table_z, factor)
        + mixed_dot("nzoxy,io->nzixy", grad_pre, point_weight)
    ).astype(jnp.bfloat16)
    point_terms = factor * mixed_dot("nzixy,nzoxy->io", layer_input, grad_pre)
    bias_terms = factor * jnp.sum(grad_pre, axis=(0, 1, 3, 4), dtype=jnp.float32)
    point_grad, bias_grad = lax.psum((point_terms, bias_terms), ("dp", "mp"))
    spec_grad = lax.psum(
        weight_terms(spectrum, grad_spectrum, mode_scale).astype(jnp.bfloat16), "dp"
    ).astype(jnp.float32)
    return (input_grad, spec_grad, point_grad, bias_grad)


def solution(mesh):
    placed = (
        P("dp", "mp", None, None, None),
        P("dp", "mp", None, None, None),
        P(None, None, None, None, "mp"),
        P(),
        P(),
    )
    return jax.shard_map(
        shards,
        mesh=mesh,
        in_specs=placed,
        out_specs=(P("dp", "mp", None, None, None), P(None, None, None, None, "mp"), P(), P()),
        check_vma=False,
    )
```

profile of v0, /device:TPU:0, one launch (start us, length us, event | category | flops | bytes accessed | tf_op | source)
XLA Modules:
  0.0 110.1 jit_solution(4023835771451078023)
XLA Ops:
  0.8 0.3 copy-done.21
  1.2 0.5 copy-done
  1.7 0.6 convolution_bitcast_fusion.7
  2.2 0.2 fusion.47
  2.8 0.4 copy.94
  3.2 1.2 %reshape.756 = bf16[32,2,512]{2,1,0:T(2,128)(2,1)} reshape(bf16[1024,1,1,2,16]{4,3,2,1,0:T(2,128)(2,1)S(1)} %bitcast.316) | data formatting | bytes 131072
  4.4 7.3 %all-to-all-start = ((bf16[32,2,512]{2,1,0:T(2,128)(2,1)}), bf16[32,2,512]{2,1,0:T(2,128)(2,1)S(1)}, u32[]{:S(2)}, u32[]{:S(2)}) async-start(bf16[32,2,512]{2,1,0:T(2,128)(2,1)} %reshape.756), calls=%async_computation | async-start | bytes 131072 | tf_op jit(solution)/shard_map/all_to_all | solution.py:42
  11.8 4.2 %fusion.120 = (bf16[16,16,16,1,32]{4,3,2,1,0:T(2,128)(2,1)}, bf16[16,16,16,1,32]{4,3,2,1,0:T(2,128)(2,1)}) fusion(bf16[16,16,16,2,32]{4,3,2,1,0:T(2,128)(2,1)S(1)} %copy-done.1), kind=kLoop, calls=%fused_computation.210 | loop fusion | bytes 1048576 | tf_op jit(solution)/shard_map/slice | solution.py:77
  16.0 1.4 %fusion.30 = f32[16,128,128]{2,0,1:T(8,128)} fusion(bf16[16,128,128]{2,1,0:T(8,128)(2,1)S(1)} %bitcast.311, bf16[16,16]{1,0:T(8,128)(2,1)S(1)} %copy-done.17), kind=kOutput, calls=%fused_computation.57 | convolution fusion | flops 8388608 | bytes 1573376 | tf_op jit(solution)/shard_map/nzixy,io->nzoxy/dot_general | solution.py:12
  17.4 0.5 compare_select_fusion.1
  18.0 1.1 %all-to-all-done = bf16[32,2,512]{2,1,0:T(2,128)(2,1)S(1)} async-done(((bf16[32,2,512]{2,1,0:T(2,128)(2,1)}), bf16[32,2,512]{2,1,0:T(2,128)(2,1)S(1)}, u32[]{:S(2)}, u32[]{:S(2)}) %all-to-all-start) | async-done | bytes 65568 | tf_op jit(solution)/shard_map/all_to_all | solution.py:42
  19.1 0.4 reshape.757
  19.5 0.6 copy.193
  20.2 0.2 convolution_bitcast_fusion.6
  20.6 0.5 copy-done.2
  21.1 4.1 %fusion.3 = (f32[16,32,16]{1,2,0:T(8,128)S(1)}, f32[16,32,16]{1,2,0:T(8,128)S(1)}, f32[16,32,16]{1,2,0:T(8,128)S(1)}, f32[16,32,16]{1,2,0:T(8,128)S(1)}, bf16[16...) fusion(f32[16,32,16]{1,2,0:T(8,128)S(1)} %copy.207, f32[16,32,16]{1,2,0:T(8,128)S(1)} %copy.206, ...), kind=kLoop, calls=%fused_computation.12 | loop fusion | flops 1277952 | bytes 1245184
  25.5 0.3 convolution_bitcast_fusion.3
  26.1 0.9 reshape.758
  27.0 4.7 %all-to-all-start.1 = ((bf16[32,2,512]{2,1,0:T(2,128)(2,1)}), bf16[32,2,512]{2,1,0:T(2,128)(2,1)S(1)}, u32[]{:S(2)}, u32[]{:S(2)}) async-start(bf16[32,2,512]{2,1,0:T(2,128)(2,1)} %reshape.758), calls=%async_computation.1 | async-start | bytes 131072 | tf_op jit(solution)/shard_map/all_to_all | solution.py:62
  31.9 0.7 copy.120
  32.6 6.5 %all-to-all-done.1 = bf16[32,2,512]{2,1,0:T(2,128)(2,1)S(1)} async-done(((bf16[32,2,512]{2,1,0:T(2,128)(2,1)}), bf16[32,2,512]{2,1,0:T(2,128)(2,1)S(1)}, u32[]{:S(2)}, u32[]{:S(2)}) %all-to-all-start.1) | async-done | bytes 65568 | tf_op jit(solution)/shard_map/all_to_all | solution.py:62
  39.1 0.2 reshape.759
  39.3 0.3 copy.101
  39.6 0.3 convolution_bitcast_fusion.2
  40.0 1.3 %convert_reduce_fusion = (f32[16]{0:T(128)S(1)}, bf16[1,1,16,128,128]{4,3,2,1,0:T(8,128)(2,1)S(1)}) fusion(f32[16]{0:T(128)S(1)} %copy-done.24, f32[16,128,128]{2,0,1:T(8,128)S(1)} %copy-done.5, bf16[128,32]{0,1:T(8,128)(2,1)S(1)} %get-tuple-element.59, bf16[128,32]{0,1:T(8,128)(2,1)S(1)} %get-tuple-element.58, bf16[16,128,32]{1,2,0:T(8,128)(2,1)S(1)} %fusion.69, ...), kind=kOutput, calls=%fused_computation.52 | convolution fusion | flops 40665072 | bytes 2375808 | tf_op jit(solution)/shard_map/nzcxk,yk->nzcxy/dot_general | solution.py:12
  41.3 0.6 convolution_bitcast_fusion.5
  41.9 0.7 fusion.17
  42.6 0.4 fusion.27
  43.0 0.2 fusion.39
  43.6 0.4 copy.107
  44.0 1.2 %reshape.760 = bf16[32,2,512]{2,1,0:T(2,128)(2,1)} reshape(bf16[1024,1,1,2,16]{4,3,2,1,0:T(2,128)(2,1)S(1)} %bitcast.318) | data formatting | bytes 131072
  45.2 2.6 %all-to-all-start.2 = ((bf16[32,2,512]{2,1,0:T(2,128)(2,1)}), bf16[32,2,512]{2,1,0:T(2,128)(2,1)S(1)}, u32[]{:S(2)}, u32[]{:S(2)}) async-start(bf16[32,2,512]{2,1,0:T(2,128)(2,1)} %reshape.760), calls=%async_computation.2 | async-start | bytes 131072 | tf_op jit(solution)/shard_map/all_to_all | solution.py:42
  47.8 40.8 %all-reduce = (f32[16,16]{0,1:T(8,128)S(1)}, f32[16]{0:T(128)}) all-reduce(f32[16,16]{0,1:T(8,128)S(1)} %fusion.17, f32[16]{0:T(128)S(1)} %broadcast_multiply_fusion), channel_id=1, replica_groups=mesh['dp'=1,'mp'=32] {'dp','mp'}, use_global_device_ids=true, to_apply=%region_0.1 | all-reduce | flops 272 | bytes 2176 | tf_op jit(solution)/shard_map/psum | solution.py:139
  88.6 0.7 copy.124
  89.3 0.4 reshape.761
  89.7 0.6 copy.195
  90.3 1.0 convolution_bitcast_fusion.4
  91.6 2.2 %fusion.7 = (f32[16,32,16]{1,2,0:T(8,128)S(1)}, f32[16,32,16]{1,2,0:T(8,128)S(1)}, f32[16,32,16]{1,2,0:T(8,128)S(1)}, f32[16,32,16]{1,2,0:T(8,128)S(1)}) fusion(f32[16,32,16]{1,2,0:T(8,128)S(1)} %copy.209, bf16[16,16,16,1,32]{4,2,1,0,3:T(8,128)(2,1)S(1)} %copy-done.4, f32[16,32,16]{1,2,0:T(8,128)S(1)} %copy.208, bf16[16,16,16,1,32]{4,2,1,0,3:T(8,128)(2,1)S(1)} %copy-done.3), kind=kLoop, calls=%fused_computation.16 | loop fusion | flops 1277952 | bytes 720896
  94.1 0.3 convolution_bitcast_fusion.1
  94.8 0.9 reshape.762
  95.6 4.8 %all-to-all-start.3 = ((bf16[32,2,512]{2,1,0:T(2,128)(2,1)}), bf16[32,2,512]{2,1,0:T(2,128)(2,1)S(1)}, u32[]{:S(2)}, u32[]{:S(2)}) async-start(bf16[32,2,512]{2,1,0:T(2,128)(2,1)} %reshape.762), calls=%async_computation.3 | async-start | bytes 131072 | tf_op jit(solution)/shard_map/all_to_all | solution.py:62
  100.5 0.6 multiply_add_fusion
  101.1 6.0 %fusion.9 = f32[16,16,16,2,32]{4,3,2,1,0:T(2,128)} fusion(f32[16,16,16,1,32]{4,3,2,1,0:T(1,128)S(1)} %bitcast.313, f32[16,16,16,1,32]{4,3,2,1,0:T(1,128)S(1)} %bitcast.312, f32[16]{0:T(128)S(1)} %copy-done.20), kind=kLoop, calls=%fused_computation.20 | loop fusion | flops 1048576 | bytes 2097216 | tf_op jit(solution)/shard_map/convert_element_type | solution.py:142
  107.1 0.8 all-to-all-done.3
  107.9 0.2 reshape.763
  108.1 0.3 copy.112
  108.4 0.3 convolution_bitcast_fusion
  108.8 1.4 %fusion.14 = bf16[1,1,16,128,128]{4,3,2,1,0:T(8,128)(2,1)} fusion(f32[128,128,16]{1,2,0:T(8,128)S(1)} %fusion.27, bf16[16,128,32]{1,2,0:T(8,128)(2,1)S(1)} %fusion.73, bf16[16,128,32]{1,2,0:T(8,128)(2,1)S(1)} %fusion.72, bf16[128,32]{0,1:T(8,128)(2,1)S(1)} %get-tuple-element.59, bf16[128,32]{0,1:T(8,128)(2,1)S(1)} %get-tuple-element.58), kind=kOutput, calls=%fused_computation.33 | convolution fusion | flops 34897920 | bytes 1851392 | tf_op jit(solution)/shard_map/nzcxk,yk->nzcxy/dot_general | solution.py:12
  (89 shorter events, 2.8 us)
Async XLA Ops:
  0.6 1.0 copy-start
  0.7 0.5 copy-start.21
  0.7 11.1 %copy-start.1 = (bf16[16,16,16,2,32]{4,3,2,1,0:T(2,128)(2,1)S(1)}, bf16[16,16,16,2,32]{4,3,2,1,0:T(2,128)(2,1)}, u32[]{:S(2)}) copy-start(bf16[16,16,16,2,32]{4,3,2,1,0:T(2,128)(2,1)} %param.7) | copy-start | bytes 1572868
  4.4 14.7 %all-to-all-start = ((bf16[32,2,512]{2,1,0:T(2,128)(2,1)}), bf16[32,2,512]{2,1,0:T(2,128)(2,1)S(1)}, u32[]{:S(2)}, u32[]{:S(2)}) async-start(bf16[32,2,512]{2,1,0:T(2,128)(2,1)} %reshape.756), calls=%async_computation | async-start | bytes 131072 | tf_op jit(solution)/shard_map/all_to_all | solution.py:42
  11.8 13.6 %copy-start.11 = (bf16[32,1,16]{0,2,1:T(8,128)(2,1)}, bf16[32,1,16]{0,2,1:T(8,128)(2,1)S(1)}, u32[]{:S(2)}) copy-start(bf16[32,1,16]{0,2,1:T(8,128)(2,1)S(1)} %get-tuple-element.64) | copy-start | bytes 3076
  11.8 13.6 %copy-start.13 = (bf16[32,1,16]{0,2,1:T(8,128)(2,1)}, bf16[32,1,16]{0,2,1:T(8,128)(2,1)S(1)}, u32[]{:S(2)}) copy-start(bf16[32,1,16]{0,2,1:T(8,128)(2,1)S(1)} %get-tuple-element.65) | copy-start | bytes 3076
  11.8 4.2 %copy-start.17 = (bf16[16,16]{1,0:T(8,128)(2,1)S(1)}, bf16[16,16]{1,0:T(8,128)(2,1)}, u32[]{:S(2)}) copy-start(bf16[16,16]{1,0:T(8,128)(2,1)} %param.8) | copy-start | bytes 1540
  18.0 2.4 %copy-start.15 = (bf16[32,16]{0,1:T(8,128)(2,1)}, bf16[32,16]{0,1:T(8,128)(2,1)S(1)}, u32[]{:S(2)}) copy-start(bf16[32,16]{0,1:T(8,128)(2,1)S(1)} %get-tuple-element.62) | copy-start | bytes 3076
  18.0 2.4 %copy-start.16 = (bf16[32,16]{0,1:T(8,128)(2,1)}, bf16[32,16]{0,1:T(8,128)(2,1)S(1)}, u32[]{:S(2)}) copy-start(bf16[32,16]{0,1:T(8,128)(2,1)S(1)} %get-tuple-element.63) | copy-start | bytes 3076
  19.5 1.6 %copy-start.2 = (bf16[16,16,16,1,32]{4,3,2,1,0:T(2,128)(2,1)S(1)}, bf16[16,16,16,1,32]{4,3,2,1,0:T(2,128)(2,1)}, u32[]{:S(2)}) copy-start(bf16[16,16,16,1,32]{4,3,2,1,0:T(2,128)(2,1)} %get-tuple-element.36) | copy-start | bytes 786436
  21.1 4.4 %copy-start.19 = (f32[16]{0:T(128)S(1)}, f32[16]{0:T(128)}, u32[]{:S(2)}) copy-start(f32[16]{0:T(128)} %compare_select_fusion.1) | copy-start | bytes 196
  25.4 6.2 %copy-start.22 = (s32[32]{0:T(128)S(1)}, s32[32]{0:T(128)}, u32[]{:S(2)}) copy-start(s32[32]{0:T(128)} %copy-done.21) | copy-start | bytes 388
  26.9 13.0 %copy-start.5 = (f32[16,128,128]{2,0,1:T(8,128)S(1)}, f32[16,128,128]{2,0,1:T(8,128)}, u32[]{:S(2)}) copy-start(f32[16,128,128]{2,0,1:T(8,128)} %fusion.30) | copy-start | bytes 3145732
  26.9 13.0 %copy-start.23 = (bf16[1,1,16,128,128]{4,3,2,1,0:T(8,128)(2,1)S(1)}, bf16[1,1,16,128,128]{4,3,2,1,0:T(8,128)(2,1)}, u32[]{:S(2)}) copy-start(bf16[1,1,16,128,128]{4,3,2,1,0:T(8,128)(2,1)} %param.6) | copy-start | bytes 1572868
  26.9 13.0 %copy-start.24 = (f32[16]{0:T(128)S(1)}, f32[16]{0:T(128)}, u32[]{:S(2)}) copy-start(f32[16]{0:T(128)} %param.9) | copy-start | bytes 196
  27.0 12.1 %all-to-all-start.1 = ((bf16[32,2,512]{2,1,0:T(2,128)(2,1)}), bf16[32,2,512]{2,1,0:T(2,128)(2,1)S(1)}, u32[]{:S(2)}, u32[]{:S(2)}) async-start(bf16[32,2,512]{2,1,0:T(2,128)(2,1)} %reshape.758), calls=%async_computation.1 | async-start | bytes 131072 | tf_op jit(solution)/shard_map/all_to_all | solution.py:62
  31.8 9.5 %copy-start.7 = (bf16[128,1,32]{0,2,1:T(8,128)(2,1)}, bf16[128,1,32]{0,2,1:T(8,128)(2,1)S(1)}, u32[]{:S(2)}) copy-start(bf16[128,1,32]{0,2,1:T(8,128)(2,1)S(1)} %get-tuple-element.56) | copy-start | bytes 24580
  31.8 9.5 %copy-start.9 = (bf16[128,1,32]{0,2,1:T(8,128)(2,1)}, bf16[128,1,32]{0,2,1:T(8,128)(2,1)S(1)}, u32[]{:S(2)}) copy-start(bf16[128,1,32]{0,2,1:T(8,128)(2,1)S(1)} %get-tuple-element.57) | copy-start | bytes 24580
  41.3 1.3 %copy-start.18 = (bf16[16,16]{1,0:T(8,128)(2,1)S(1)}, bf16[16,16]{1,0:T(8,128)(2,1)}, u32[]{:S(2)}) copy-start(bf16[16,16]{1,0:T(8,128)(2,1)} %param.8) | copy-start | bytes 1540
  45.2 44.1 %all-to-all-start.2 = ((bf16[32,2,512]{2,1,0:T(2,128)(2,1)}), bf16[32,2,512]{2,1,0:T(2,128)(2,1)S(1)}, u32[]{:S(2)}, u32[]{:S(2)}) async-start(bf16[32,2,512]{2,1,0:T(2,128)(2,1)} %reshape.760), calls=%async_computation.2 | async-start | bytes 131072 | tf_op jit(solution)/shard_map/all_to_all | solution.py:42
  89.7 1.9 %copy-start.3 = (bf16[16,16,16,1,32]{4,2,1,0,3:T(8,128)(2,1)S(1)}, bf16[16,16,16,1,32]{4,2,1,0,3:T(8,128)(2,1)}, u32[]{:S(2)}) copy-start(bf16[16,16,16,1,32]{4,2,1,0,3:T(8,128)(2,1)} %get-tuple-element.34) | copy-start | bytes 786436
  90.3 1.3 %copy-start.4 = (bf16[16,16,16,1,32]{4,2,1,0,3:T(8,128)(2,1)S(1)}, bf16[16,16,16,1,32]{4,2,1,0,3:T(8,128)(2,1)}, u32[]{:S(2)}) copy-start(bf16[16,16,16,1,32]{4,2,1,0,3:T(8,128)(2,1)} %get-tuple-element.35) | copy-start | bytes 786436
  91.5 2.6 %copy-start.12 = (bf16[32,1,16]{0,2,1:T(8,128)(2,1)S(1)}, bf16[32,1,16]{0,2,1:T(8,128)(2,1)}, u32[]{:S(2)}) copy-start(bf16[32,1,16]{0,2,1:T(8,128)(2,1)} %copy-done.11) | copy-start | bytes 3076
  91.5 2.6 %copy-start.14 = (bf16[32,1,16]{0,2,1:T(8,128)(2,1)S(1)}, bf16[32,1,16]{0,2,1:T(8,128)(2,1)}, u32[]{:S(2)}) copy-start(bf16[32,1,16]{0,2,1:T(8,128)(2,1)} %copy-done.13) | copy-start | bytes 3076
  91.5 2.6 %copy-start.20 = (f32[16]{0:T(128)S(1)}, f32[16]{0:T(128)}, u32[]{:S(2)}) copy-start(f32[16]{0:T(128)} %compare_select_fusion.1) | copy-start | bytes 196
  94.1 6.4 %copy-start.6 = (f32[16,32,16]{1,2,0:T(8,128)S(1)}, f32[16,32,16]{1,2,0:T(8,128)}, u32[]{:S(2)}) copy-start(f32[16,32,16]{1,2,0:T(8,128)} %copy.120) | copy-start | bytes 98308
  95.6 12.2 %all-to-all-start.3 = ((bf16[32,2,512]{2,1,0:T(2,128)(2,1)}), bf16[32,2,512]{2,1,0:T(2,128)(2,1)S(1)}, u32[]{:S(2)}, u32[]{:S(2)}) async-start(bf16[32,2,512]{2,1,0:T(2,128)(2,1)} %reshape.762), calls=%async_computation.3 | async-start | bytes 131072 | tf_op jit(solution)/shard_map/all_to_all | solution.py:62
  101.1 7.3 %copy-start.8 = (bf16[128,1,32]{0,2,1:T(8,128)(2,1)S(1)}, bf16[128,1,32]{0,2,1:T(8,128)(2,1)}, u32[]{:S(2)}) copy-start(bf16[128,1,32]{0,2,1:T(8,128)(2,1)} %copy-done.7) | copy-start | bytes 24580
  101.1 7.3 %copy-start.10 = (bf16[128,1,32]{0,2,1:T(8,128)(2,1)S(1)}, bf16[128,1,32]{0,2,1:T(8,128)(2,1)}, u32[]{:S(2)}) copy-start(bf16[128,1,32]{0,2,1:T(8,128)(2,1)} %copy-done.9) | copy-start | bytes 24580
where the time goes:
time: 111 us; the launch traced here: 110 us
  blocking collectives  40.8 us (37%)
  starting transfers between devices  19.4 us (17%)
  local copies, waits for them, and re-layouts  16.2 us (15%)
  other arithmetic  15.3 us (14%)
  matrix products  8.76 us (8%)
  waiting for transfers between devices  8.38 us (8%)
  between operations  1.33 us (1%)
    psum x1, blocking collectives, shards(): point_grad, bias_grad = lax.psum((point_terms, bias_terms), ('dp', 'mp'))  40.8 us
    all_to_all x2, starting transfers between devices, to_spectrum(): lax.all_to_all(planes, 'mp', split_axis=4, concat_axis=1, tiled=True)  9.86 us
    all_to_all x2, starting transfers between devices, to_field(): lax.all_to_all(pencil_data, 'mp', split_axis=1, concat_axis=4, tiled=True)  9.53 us
    dot_general x13, matrix products, mixed_dot(): jnp.einsum(formula, first_op, second_op, preferred_element_type=jnp.float32)  8.76 us
    unnamed x63, local copies, waits for them, and re-layouts  7.58 us
    all_to_all x2, waiting for transfers between devices, to_field(): lax.all_to_all(pencil_data, 'mp', split_axis=1, concat_axis=4, tiled=True)  7.25 us
    unnamed x2, other arithmetic  6.34 us
    convert_element_type x1, other arithmetic, shards(): spec_grad = lax.psum(weight_terms(spectrum, grad_spectrum, mode_scale).as...  6 us
  transfers between devices with their start and end apart: 4, of which 3 were waited for; matrix products, arithmetic and copies ran while one was open for 13% of the time, Pallas kernels for 0%

commit v1 on v0

--- a/solution.py
+++ b/solution.py
@@ -23,7 +23,15 @@
     return jnp.concatenate([jnp.cos(phases), -jnp.sin(phases)], axis=1).astype(jnp.bfloat16)
 
 
-def to_spectrum(values, table_x, table_y, table_z, factor):
+def split3(value):
+    high = value.astype(jnp.bfloat16)
+    rest = value - high.astype(jnp.float32)
+    mid = rest.astype(jnp.bfloat16)
+    low = (rest - mid.astype(jnp.float32)).astype(jnp.bfloat16)
+    return jnp.stack([high, mid, low])
+
+
+def to_spectrum(values, table_x, table_y, table_z, factor, extra=None):
     samples, local_z, channels = (values.shape[0], values.shape[1], values.shape[2])
     half_x = table_x.shape[1] // 2
     half_y = table_y.shape[1] // 2
@@ -37,14 +45,33 @@
         .reshape(samples, local_z, channels, 2, half_x * half_y)
         .astype(jnp.bfloat16)
     )
-    whole_z = mixed_dot(
-        "nzcrp,zk->nkcrp",
-        lax.all_to_all(planes, "mp", split_axis=4, concat_axis=1, tiled=True),
-        table_z,
-    )
+    shards_mp = lax.axis_size("mp")
+    width = half_x * half_y // shards_mp
+    total = None
+    if extra is not None:
+        size = extra.size
+        cells = samples * local_z * channels * 2
+        more = -(-3 * size // cells)
+        flat = jnp.pad(split3(extra).reshape(-1), (0, cells * more - 3 * size))
+        flat = jnp.broadcast_to(
+            flat.reshape(samples, local_z, channels, 2, 1, more),
+            (samples, local_z, channels, 2, shards_mp, more),
+        )
+        planes = jnp.concatenate(
+            [planes.reshape(samples, local_z, channels, 2, shards_mp, width), flat], axis=5
+        ).reshape(samples, local_z, channels, 2, shards_mp * (width + more))
+    planes = lax.all_to_all(planes, "mp", split_axis=4, concat_axis=1, tiled=True)
+    if extra is not None:
+        tail = planes[..., width:].astype(jnp.float32)
+        tail = tail.reshape(samples, shards_mp, local_z, channels, 2, more)
+        tail = jnp.transpose(tail, (1, 0, 2, 3, 4, 5)).reshape(shards_mp, -1)
+        total = jnp.sum(jnp.sum(tail, axis=0)[: 3 * size].reshape(3, size), axis=0)
+        planes = planes[..., :width]
+    whole_z = mixed_dot("nzcrp,zk->nkcrp", planes, table_z)
     real_z = whole_z[:, :half_z, :, 0] - whole_z[:, half_z:, :, 1]
     imag_z = whole_z[:, :half_z, :, 1] + whole_z[:, half_z:, :, 0]
-    return (factor * jnp.stack([real_z, imag_z], axis=3)).astype(jnp.bfloat16)
+    result = (factor * jnp.stack([real_z, imag_z], axis=3)).astype(jnp.bfloat16)
+    return result if extra is None else (result, total)
 
 
 def to_field(spectrum, table_x, table_y, table_z, factor):
@@ -128,15 +155,19 @@
         + bias_term[None, None, :, None, None]
     )
     grad_pre = (cotangent.astype(jnp.float32) * gelu_slope(pre_act)).astype(jnp.bfloat16)
-    grad_spectrum = to_spectrum(grad_pre, table_x, table_y, table_z, factor)
+    point_terms = factor * mixed_dot("nzixy,nzoxy->io", layer_input, grad_pre)
+    bias_terms = factor * jnp.sum(grad_pre, axis=(0, 1, 3, 4), dtype=jnp.float32)
+    terms = jnp.concatenate([point_terms, bias_terms[None]], axis=0)
+    grad_spectrum, terms_sum = to_spectrum(
+        grad_pre, table_x, table_y, table_z, factor, terms.reshape(-1)
+    )
+    terms_sum = lax.psum(terms_sum.reshape(terms.shape), "dp")
+    point_grad, bias_grad = terms_sum[:-1], terms_sum[-1]
     back_spec = back_modes(grad_spectrum, spec_weight, mode_scale)
     input_grad = (
         to_field(back_spec, table_x, table_y, table_z, factor)
         + mixed_dot("nzoxy,io->nzixy", grad_pre, point_weight)
     ).astype(jnp.bfloat16)
-    point_terms = factor * mixed_dot("nzixy,nzoxy->io", layer_input, grad_pre)
-    bias_terms = factor * jnp.sum(grad_pre, axis=(0, 1, 3, 4), dtype=jnp.float32)
-    point_grad, bias_grad = lax.psum((point_terms, bias_terms), ("dp", "mp"))
     spec_grad = lax.psum(
         weight_terms(spectrum, grad_spectrum, mode_scale).astype(jnp.bfloat16), "dp"
     ).astype(jnp.float32)

time: 111 us -> 79.3 us (0.71)
  blocking collectives: 40.8 us -> 0 us
  waiting for transfers between devices: 8.38 us -> 16.5 us
  local copies, waits for them, and re-layouts: 16.2 us -> 21.3 us
  starting transfers between devices: 19.4 us -> 16.8 us
    psum x1 -> x0, blocking collectives: 40.8 us -> none  [shards(): point_grad, bias_grad = lax.psum((point_terms, bias_terms), ('dp', 'mp'))]
    all_to_all x2, waiting for transfers between devices: 1.14 us -> 9.33 us  [to_spectrum(): lax.all_to_all(planes, 'mp', split_axis=4, concat_axis=1, tiled=True)]
    all_to_all x2, starting transfers between devices: 9.53 us -> 6.72 us  [to_field(): lax.all_to_all(pencil_data, 'mp', split_axis=1, concat_axis=4, tiled=True)]
    all_to_all x2, local copies, waits for them, and re-layouts: 1.27 us -> 3.24 us  [to_spectrum(): lax.all_to_all(planes, 'mp', split_axis=4, concat_axis=1, tiled=True)]
    unnamed x63 -> x30, local copies, waits for them, and re-layouts: 7.58 us -> 9.28 us
    slice x0 -> x3, local copies, waits for them, and re-layouts: none -> 1.2 us  [shards(): point_grad, bias_grad = (terms_sum[:-1], terms_sum[-1])]
    reshape x0 -> x4, local copies, waits for them, and re-layouts: none -> 1.15 us  [the longest x1 0.9 us: to_spectrum(): planes = jnp.concatenate([planes.reshape(samples, local_z, channels, 2, s...]
  transfers between devices with their start and end apart: 4 -> 4, of which waited for: 3 -> 3; matrix products, arithmetic and copies ran while one was open for 13% -> 18% of each run, Pallas kernels for 0% -> 0%
where the time goes in v1:
time: 79.3 us; the launch traced here: 78.9 us
  local copies, waits for them, and re-layouts  21.3 us (27%)
  starting transfers between devices  16.8 us (21%)
  waiting for transfers between devices  16.5 us (21%)
  other arithmetic  15.3 us (19%)
  matrix products  7.95 us (10%)
  between operations  1.15 us (1%)
    all_to_all x2, starting transfers between devices, to_spectrum(): lax.all_to_all(planes, 'mp', split_axis=4, concat_axis=1, tiled=True)  10.1 us
    all_to_all x2, waiting for transfers between devices, to_spectrum(): lax.all_to_all(planes, 'mp', split_axis=4, concat_axis=1, tiled=True)  9.33 us
    unnamed x30, local copies, waits for them, and re-layouts  9.28 us
    dot_general x13, matrix products, mixed_dot(): jnp.einsum(formula, first_op, second_op, preferred_element_type=jnp.float32)  7.95 us
    all_to_all x2, waiting for transfers between devices, to_field(): lax.all_to_all(pencil_data, 'mp', split_axis=1, concat_axis=4, tiled=True)  7.15 us
    all_to_all x2, starting transfers between devices, to_field(): lax.all_to_all(pencil_data, 'mp', split_axis=1, concat_axis=4, tiled=True)  6.72 us
    unnamed x2, other arithmetic  6.38 us
    convert_element_type x1, other arithmetic, shards(): spec_grad = lax.psum(weight_terms(spectrum, grad_spectrum, mode_scale).as...  6 us
  transfers between devices with their start and end apart: 4, of which 3 were waited for; matrix products, arithmetic and copies ran while one was open for 18% of the time, Pallas kernels for 0%

profile of v1, /device:TPU:0, one launch (start us, length us, event | category | flops | bytes accessed | tf_op | source)
XLA Modules:
  0.0 78.9 jit_solution(17388587552800232085)
XLA Ops:
  0.8 0.9 %copy-done = bf16[1,1,16,128,128]{4,3,2,1,0:T(8,128)(2,1)S(1)} copy-done((bf16[1,1,16,128,128]{4,3,2,1,0:T(8,128)(2,1)S(1)}, bf16[1,1,16,128,128]{4,3,2,1,0:T(8,128)(2,1)}, u32[]{:S(2)}) %copy-start) | copy-done | bytes 524312
  1.7 0.6 convolution_bitcast_fusion.7
  2.2 0.2 fusion.47
  2.5 0.2 stack.79
  2.8 0.4 copy.130
  3.2 1.2 %reshape.845 = bf16[32,2,512]{2,1,0:T(2,128)(2,1)} reshape(bf16[1024,1,1,2,16]{4,3,2,1,0:T(2,128)(2,1)S(1)} %bitcast.325) | data formatting | bytes 131072
  4.4 7.3 %all-to-all-start = ((bf16[32,2,512]{2,1,0:T(2,128)(2,1)}), bf16[32,2,512]{2,1,0:T(2,128)(2,1)S(1)}, u32[]{:S(2)}, u32[]{:S(2)}) async-start(bf16[32,2,512]{2,1,0:T(2,128)(2,1)} %reshape.845), calls=%async_computation | async-start | bytes 131072 | tf_op jit(solution)/shard_map/all_to_all | solution.py:63
  11.8 4.2 %fusion.122 = (bf16[16,16,16,1,32]{4,3,2,1,0:T(2,128)(2,1)}, bf16[16,16,16,1,32]{4,3,2,1,0:T(2,128)(2,1)}) fusion(bf16[16,16,16,2,32]{4,3,2,1,0:T(2,128)(2,1)S(1)} %copy-done.1), kind=kLoop, calls=%fused_computation.218 | loop fusion | bytes 1048576 | tf_op jit(solution)/shard_map/slice | solution.py:104
  16.0 1.4 %fusion.30 = f32[16,128,128]{2,0,1:T(8,128)} fusion(bf16[16,128,128]{2,1,0:T(8,128)(2,1)S(1)} %bitcast.316, bf16[16,16]{1,0:T(8,128)(2,1)S(1)} %copy-done.6), kind=kOutput, calls=%fused_computation.58 | convolution fusion | flops 8388608 | bytes 1573376 | tf_op jit(solution)/shard_map/nzixy,io->nzoxy/dot_general | solution.py:12
  17.5 1.7 %all-to-all-done = bf16[32,2,512]{2,1,0:T(2,128)(2,1)S(1)} async-done(((bf16[32,2,512]{2,1,0:T(2,128)(2,1)}), bf16[32,2,512]{2,1,0:T(2,128)(2,1)S(1)}, u32[]{:S(2)}, u32[]{:S(2)}) %all-to-all-start) | async-done | bytes 65568 | tf_op jit(solution)/shard_map/all_to_all | solution.py:63
  19.1 0.4 reshape.846
  19.5 0.6 copy.231
  20.2 0.2 convolution_bitcast_fusion.6
  20.6 0.5 copy-done.2
  21.1 4.1 %fusion.3 = (f32[16,32,16]{1,2,0:T(8,128)S(1)}, f32[16,32,16]{1,2,0:T(8,128)S(1)}, f32[16,32,16]{1,2,0:T(8,128)S(1)}, f32[16,32,16]{1,2,0:T(8,128)S(1)}, bf16[16...) fusion(f32[16,32,16]{1,2,0:T(8,128)S(1)} %copy.246, f32[16,32,16]{1,2,0:T(8,128)S(1)} %copy.245, ...), kind=kLoop, calls=%fused_computation.12 | loop fusion | flops 1277952 | bytes 1245184
  25.4 0.3 convolution_bitcast_fusion.3
  26.0 0.9 %reshape.847 = bf16[32,2,512]{2,1,0:T(2,128)(2,1)} reshape(bf16[32,1,2,16,32]{4,3,2,1,0:T(8,128)(2,1)S(1)} %bitcast.327) | data formatting | bytes 131072
  26.9 4.1 %all-to-all-start.1 = ((bf16[32,2,512]{2,1,0:T(2,128)(2,1)}), bf16[32,2,512]{2,1,0:T(2,128)(2,1)S(1)}, u32[]{:S(2)}, u32[]{:S(2)}) async-start(bf16[32,2,512]{2,1,0:T(2,128)(2,1)} %reshape.847), calls=%async_computation.1 | async-start | bytes 131072 | tf_op jit(solution)/shard_map/all_to_all | solution.py:89
  31.3 7.1 %all-to-all-done.1 = bf16[32,2,512]{2,1,0:T(2,128)(2,1)S(1)} async-done(((bf16[32,2,512]{2,1,0:T(2,128)(2,1)}), bf16[32,2,512]{2,1,0:T(2,128)(2,1)S(1)}, u32[]{:S(2)}, u32[]{:S(2)}) %all-to-all-start.1) | async-done | bytes 65568 | tf_op jit(solution)/shard_map/all_to_all | solution.py:89
  38.5 0.2 reshape.848
  38.7 0.3 copy.137
  39.0 0.3 convolution_bitcast_fusion.2
  39.4 1.3 %convert_reduce_fusion = (f32[16]{0:T(128)S(1)}, bf16[1,1,16,128,128]{4,3,2,1,0:T(8,128)(2,1)S(1)}) fusion(f32[16]{0:T(128)S(1)} %copy-done.8, f32[16,128,128]{2,0,1:T(8,128)S(1)} %copy-done.5, bf16[128,32]{0,1:T(8,128)(2,1)S(1)} %get-tuple-element.44, bf16[128,32]{0,1:T(8,128)(2,1)S(1)} %get-tuple-element.43, bf16[16,128,32]{1,2,0:T(8,128)(2,1)S(1)} %fusion.68, ...), kind=kOutput, calls=%fused_computation.52 | convolution fusion | flops 40665072 | bytes 2375808 | tf_op jit(solution)/shard_map/nzcxk,yk->nzcxy/dot_general | solution.py:12
  40.8 0.6 convolution_bitcast_fusion.5
  41.4 0.7 fusion.17
  42.6 0.2 fusion.69
  43.0 0.9 %copy.233 = bf16[1,1,16,2,32,58]{2,3,5,4,1,0:T(2,128)(2,1)S(1)} copy(bf16[1,1,16,2,32,58]{5,4,2,3,1,0:T(8,128)(2,1)S(1)} %pad_maximum_fusion.1) | data formatting | bytes 237568 | tf_op jit(solution)/shard_map/reshape | solution.py:62
  43.9 1.4 %reshape.849 = bf16[32,2,928]{2,1,0:T(2,128)(2,1)} reshape(bf16[1856,1,1,2,16]{4,3,2,1,0:T(2,128)(2,1)S(1)} %bitcast.319) | data formatting | bytes 237568
  45.3 2.8 %all-to-all-start.2 = ((bf16[32,2,928]{2,1,0:T(2,128)(2,1)}), bf16[32,2,928]{2,1,0:T(2,128)(2,1)S(1)}, u32[]{:S(2)}, u32[]{:S(2)}) async-start(bf16[32,2,928]{2,1,0:T(2,128)(2,1)} %reshape.849), calls=%async_computation.2 | async-start | bytes 262144 | tf_op jit(solution)/shard_map/all_to_all | solution.py:63
  48.1 0.4 fusion.26
  48.5 7.6 %all-to-all-done.2 = bf16[32,2,928]{2,1,0:T(2,128)(2,1)S(1)} async-done(((bf16[32,2,928]{2,1,0:T(2,128)(2,1)}), bf16[32,2,928]{2,1,0:T(2,128)(2,1)S(1)}, u32[]{:S(2)}, u32[]{:S(2)}) %all-to-all-start.2) | async-done | bytes 118816 | tf_op jit(solution)/shard_map/all_to_all | solution.py:63
  56.1 1.9 %reshape.850 = bf16[1856,1,1,2,16]{4,3,2,1,0:T(2,128)(2,1)} reshape(bf16[32,2,928]{2,1,0:T(2,128)(2,1)S(1)} %all-to-all-done.2) | data formatting | bytes 237568
  58.0 2.6 %copy.234 = bf16[1,1,16,2,32,58]{5,4,3,2,1,0:T(8,128)(2,1)S(1)} copy(bf16[1,1,16,2,32,58]{2,3,5,4,1,0:T(2,128)(2,1)} %bitcast.320) | data formatting | bytes 237568 | tf_op jit(solution)/shard_map/all_to_all | solution.py:63
  60.6 0.2 convolution_bitcast_fusion.4
  61.1 0.8 copy-done.4
  61.9 2.2 %fusion.7 = (f32[16,32,16]{1,2,0:T(8,128)S(1)}, f32[16,32,16]{1,2,0:T(8,128)S(1)}, f32[16,32,16]{1,2,0:T(8,128)S(1)}, f32[16,32,16]{1,2,0:T(8,128)S(1)}) fusion(f32[16,32,16]{1,2,0:T(8,128)S(1)} %copy.248, bf16[16,16,16,1,32]{4,2,1,0,3:T(8,128)(2,1)S(1)} %copy-done.4, f32[16,32,16]{1,2,0:T(8,128)S(1)} %copy.247, bf16[16,16,16,1,32]{4,2,1,0,3:T(8,128)(2,1)S(1)} %copy-done.3), kind=kLoop, calls=%fused_computation.16 | loop fusion | flops 1277952 | bytes 720896
  64.3 0.3 convolution_bitcast_fusion.1
  65.0 0.9 %reshape.851 = bf16[32,2,512]{2,1,0:T(2,128)(2,1)} reshape(bf16[32,1,2,16,32]{4,3,2,1,0:T(8,128)(2,1)S(1)} %bitcast.329) | data formatting | bytes 131072
  65.8 2.6 %all-to-all-start.3 = ((bf16[32,2,512]{2,1,0:T(2,128)(2,1)}), bf16[32,2,512]{2,1,0:T(2,128)(2,1)S(1)}, u32[]{:S(2)}, u32[]{:S(2)}) async-start(bf16[32,2,512]{2,1,0:T(2,128)(2,1)} %reshape.851), calls=%async_computation.3 | async-start | bytes 131072 | tf_op jit(solution)/shard_map/all_to_all | solution.py:89
  68.4 0.6 multiply_add_fusion
  69.0 6.0 %fusion.9 = f32[16,16,16,2,32]{4,3,2,1,0:T(2,128)} fusion(f32[16,16,16,1,32]{4,3,2,1,0:T(1,128)S(1)} %bitcast.318, f32[16,16,16,1,32]{4,3,2,1,0:T(1,128)S(1)} %bitcast.317, f32[16]{0:T(128)S(1)} %compare_select_fusion.1), kind=kLoop, calls=%fused_computation.20 | loop fusion | flops 1048576 | bytes 2097216 | tf_op jit(solution)/shard_map/convert_element_type | solution.py:173
  75.0 0.2 convert_reduce_fusion.1
  75.4 0.5 slice.188
  75.9 0.7 slice.187
  76.6 0.2 reshape.852
  76.8 0.3 copy.153
  77.1 0.3 convolution_bitcast_fusion
  77.5 1.4 %fusion.14 = bf16[1,1,16,128,128]{4,3,2,1,0:T(8,128)(2,1)} fusion(f32[128,128,16]{1,2,0:T(8,128)S(1)} %fusion.26, bf16[16,128,32]{1,2,0:T(8,128)(2,1)S(1)} %fusion.74, bf16[16,128,32]{1,2,0:T(8,128)(2,1)S(1)} %fusion.73, bf16[128,32]{0,1:T(8,128)(2,1)S(1)} %get-tuple-element.44, bf16[128,32]{0,1:T(8,128)(2,1)S(1)} %get-tuple-element.43), kind=kOutput, calls=%fused_computation.33 | convolution fusion | flops 34897920 | bytes 1851392 | tf_op jit(solution)/shard_map/nzcxk,yk->nzcxy/dot_general | solution.py:12
  (71 shorter events, 3.2 us)
Async XLA Ops:
  0.6 1.0 %copy-start = (bf16[1,1,16,128,128]{4,3,2,1,0:T(8,128)(2,1)S(1)}, bf16[1,1,16,128,128]{4,3,2,1,0:T(8,128)(2,1)}, u32[]{:S(2)}) copy-start(bf16[1,1,16,128,128]{4,3,2,1,0:T(8,128)(2,1)} %param.5) | copy-start | bytes 1572868
  0.7 11.1 %copy-start.1 = (bf16[16,16,16,2,32]{4,3,2,1,0:T(2,128)(2,1)S(1)}, bf16[16,16,16,2,32]{4,3,2,1,0:T(2,128)(2,1)}, u32[]{:S(2)}) copy-start(bf16[16,16,16,2,32]{4,3,2,1,0:T(2,128)(2,1)} %param.7) | copy-start | bytes 1572868
  4.4 14.7 %all-to-all-start = ((bf16[32,2,512]{2,1,0:T(2,128)(2,1)}), bf16[32,2,512]{2,1,0:T(2,128)(2,1)S(1)}, u32[]{:S(2)}, u32[]{:S(2)}) async-start(bf16[32,2,512]{2,1,0:T(2,128)(2,1)} %reshape.845), calls=%async_computation | async-start | bytes 131072 | tf_op jit(solution)/shard_map/all_to_all | solution.py:63
  11.8 4.2 %copy-start.6 = (bf16[16,16]{1,0:T(8,128)(2,1)S(1)}, bf16[16,16]{1,0:T(8,128)(2,1)}, u32[]{:S(2)}) copy-start(bf16[16,16]{1,0:T(8,128)(2,1)} %param.8) | copy-start | bytes 1540
  19.5 1.6 %copy-start.2 = (bf16[16,16,16,1,32]{4,3,2,1,0:T(2,128)(2,1)S(1)}, bf16[16,16,16,1,32]{4,3,2,1,0:T(2,128)(2,1)}, u32[]{:S(2)}) copy-start(bf16[16,16,16,1,32]{4,3,2,1,0:T(2,128)(2,1)} %get-tuple-element.18) | copy-start | bytes 786436
  26.9 12.5 %copy-start.5 = (f32[16,128,128]{2,0,1:T(8,128)S(1)}, f32[16,128,128]{2,0,1:T(8,128)}, u32[]{:S(2)}) copy-start(f32[16,128,128]{2,0,1:T(8,128)} %fusion.30) | copy-start | bytes 3145732
  26.9 12.5 %copy-start.7 = (bf16[1,1,16,128,128]{4,3,2,1,0:T(8,128)(2,1)S(1)}, bf16[1,1,16,128,128]{4,3,2,1,0:T(8,128)(2,1)}, u32[]{:S(2)}) copy-start(bf16[1,1,16,128,128]{4,3,2,1,0:T(8,128)(2,1)} %param.6) | copy-start | bytes 1572868
  26.9 12.5 %copy-start.8 = (f32[16]{0:T(128)S(1)}, f32[16]{0:T(128)}, u32[]{:S(2)}) copy-start(f32[16]{0:T(128)} %param.9) | copy-start | bytes 196
  26.9 11.6 %all-to-all-start.1 = ((bf16[32,2,512]{2,1,0:T(2,128)(2,1)}), bf16[32,2,512]{2,1,0:T(2,128)(2,1)S(1)}, u32[]{:S(2)}, u32[]{:S(2)}) async-start(bf16[32,2,512]{2,1,0:T(2,128)(2,1)} %reshape.847), calls=%async_computation.1 | async-start | bytes 131072 | tf_op jit(solution)/shard_map/all_to_all | solution.py:89
  45.3 10.8 %all-to-all-start.2 = ((bf16[32,2,928]{2,1,0:T(2,128)(2,1)}), bf16[32,2,928]{2,1,0:T(2,128)(2,1)S(1)}, u32[]{:S(2)}, u32[]{:S(2)}) async-start(bf16[32,2,928]{2,1,0:T(2,128)(2,1)} %reshape.849), calls=%async_computation.2 | async-start | bytes 262144 | tf_op jit(solution)/shard_map/all_to_all | solution.py:63
  58.0 3.1 %copy-start.3 = (bf16[16,16,16,1,32]{4,2,1,0,3:T(8,128)(2,1)S(1)}, bf16[16,16,16,1,32]{4,2,1,0,3:T(8,128)(2,1)}, u32[]{:S(2)}) copy-start(bf16[16,16,16,1,32]{4,2,1,0,3:T(8,128)(2,1)} %get-tuple-element.16) | copy-start | bytes 786436
  60.6 1.2 %copy-start.4 = (bf16[16,16,16,1,32]{4,2,1,0,3:T(8,128)(2,1)S(1)}, bf16[16,16,16,1,32]{4,2,1,0,3:T(8,128)(2,1)}, u32[]{:S(2)}) copy-start(bf16[16,16,16,1,32]{4,2,1,0,3:T(8,128)(2,1)} %get-tuple-element.17) | copy-start | bytes 786436
  65.8 10.8 %all-to-all-start.3 = ((bf16[32,2,512]{2,1,0:T(2,128)(2,1)}), bf16[32,2,512]{2,1,0:T(2,128)(2,1)S(1)}, u32[]{:S(2)}, u32[]{:S(2)}) async-start(bf16[32,2,512]{2,1,0:T(2,128)(2,1)} %reshape.851), calls=%async_computation.3 | async-start | bytes 131072 | tf_op jit(solution)/shard_map/all_to_all | solution.py:89

commit v2 on v1

--- a/solution.py
+++ b/solution.py
@@ -1,8 +1,13 @@
+import functools
 import math
 
 import jax
 import jax.numpy as jnp
+import ml_dtypes
+import numpy as np
 from jax import lax
+from jax.experimental import pallas as pl
+from jax.experimental.pallas import tpu as pltpu
 from jax.sharding import PartitionSpec as P
 
 SQRT_TWO_PI = math.sqrt(2.0 / math.pi)
@@ -137,9 +142,342 @@
     )
 
 
+def np_table(length, freq_count, signed):
+    frequency = np.arange(freq_count)
+    if signed:
+        frequency = np.where(frequency >= freq_count // 2, frequency - freq_count, frequency)
+    phases = np.mod(np.arange(length)[:, None] * frequency[None, :], length) * (
+        2.0 * math.pi / length
+    )
+    return np.cos(phases), -np.sin(phases)
+
+
+def lane_map(half, picks):
+    out = np.zeros((4 * half, 4 * half))
+    for group, (source, sign) in enumerate(picks):
+        for lane in range(half):
+            out[source * half + lane, group * half + lane] = sign
+    return out
+
+
+def fused_kernel(
+    planes, chans, cx, cy, modes, factor,
+    x_ref, cot_ref, w_ref, pw_ref, bias_ref,
+    ty1, ty2, tyi, txf, txi, kf, ki, perm, mask_ref,
+    dx_ref, sg_ref, term_ref,
+    send, recv, fbuf, jbuf, spec, gspec, wraw, wa, mix, pwise, gp, bsum,
+    send_sem, recv_sem,
+):
+    f32, bf16 = jnp.float32, jnp.bfloat16
+    me = lax.axis_index("mp")
+    n = planes
+    half = 2 * modes
+    kc = modes * chans
+    blk = 16
+
+    def dot(a, b):
+        return jnp.dot(a, b, preferred_element_type=f32)
+
+    barrier = pltpu.get_barrier_semaphore()
+
+    def greet(j, carry):
+        other = lax.rem(me + j, n)
+        pl.semaphore_signal(
+            barrier, inc=1, device_id={"mp": other}, device_id_type=pl.DeviceIdType.MESH
+        )
+        return carry
+
+    lax.fori_loop(1, n, greet, 0)
+
+    def ship(s):
+        def go(j, carry):
+            other = lax.rem(me + j, n)
+            pltpu.make_async_remote_copy(
+                src_ref=send.at[s, other],
+                dst_ref=recv.at[s, me],
+                send_sem=send_sem.at[s],
+                recv_sem=recv_sem.at[s],
+                device_id={"mp": other},
+                device_id_type=pl.DeviceIdType.MESH,
+            ).start()
+            return carry
+
+        lax.fori_loop(1, n, go, 0)
+        recv[s, me] = send[s, me]
+
+    def arrive(s):
+        part = recv.at[s, pl.ds(0, n - 1)]
+        pltpu.make_async_copy(part, part, recv_sem.at[s]).wait()
+
+    def left(s):
+        part = send.at[s, pl.ds(0, n - 1)]
+        pltpu.make_async_copy(part, part, send_sem.at[s]).wait()
+
+    def forward(src_ref, c):
+        plane = src_ref[c]
+        stacked = jnp.concatenate(
+            [dot(plane, ty1[...]).astype(bf16), dot(plane, ty2[...]).astype(bf16)], axis=0
+        )
+        fbuf[:, c, :] = dot(txf[...], stacked)
+
+    for c in range(chans):
+        forward(x_ref, c)
+    send[0] = fbuf[...].astype(bf16)
+    pl.semaphore_wait(barrier, n - 1)
+    ship(0)
+
+    def spread(k, carry):
+        rows = chans * chans
+        start = k * (2 * rows)
+        wraw[...] = w_ref[pl.ds(pl.multiple_of(start, 2 * rows), 2 * rows), :].astype(f32)
+        real = wraw[pl.ds(0, rows, stride=2), :].astype(bf16)
+        imag = wraw[pl.ds(1, rows, stride=2), :].astype(bf16)
+        wa[k] = (dot(real, perm[5][:half]) + dot(imag, perm[6][:half])).astype(bf16).reshape(
+            chans, chans, 4 * half
+        )
+        return carry
+
+    lax.fori_loop(0, modes, spread, 0)
+
+    row = lax.broadcasted_iota(jnp.int32, (chans * blk, chans), 0)
+    col = lax.broadcasted_iota(jnp.int32, (chans * blk, chans), 1)
+    rep = jnp.where(row // blk == col, 1.0, 0.0).astype(bf16)
+    mask = mask_ref[...]
+    kron_dims = (((1,), (1,)), ((), ()))
+
+    def kron(transposed):
+        if transposed:
+            tall = lax.dot_general(rep, pw_ref[...], kron_dims, preferred_element_type=f32)
+        else:
+            tall = dot(rep, pw_ref[...])
+        wide = lax.dot_general(tall.astype(bf16), rep, kron_dims, preferred_element_type=f32)
+        return (wide * mask).astype(bf16)
+
+    def pointwise(src_ref, matrix):
+        for b in range(cx // blk):
+            rows = pl.ds(b * blk, blk)
+            block = src_ref[:, rows, :].reshape(chans * blk, cy)
+            pwise[:, rows, :] = dot(matrix, block).reshape(chans, blk, cy)
+
+    pointwise(x_ref, kron(True))
+
+    def z_forward(s):
+        got = recv[s].reshape(n * chans, 4 * half)
+        turned = dot(got, perm[0]).astype(bf16)
+        return (factor * (dot(kf[0], got) + dot(kf[1], turned))).astype(bf16)
+
+    def z_inverse(s):
+        folded = mix[...] + pltpu.roll(mix[...], 2 * half, 1)
+        scale = jnp.where(
+            lax.broadcasted_iota(jnp.int32, (kc, 4 * half), 0) < chans, 1.0, 2.0
+        )
+        modes_in = (scale * folded).astype(bf16)
+        turned = dot(modes_in, perm[0]).astype(bf16)
+        out = dot(ki[0], modes_in) - dot(ki[1], turned)
+        send[s] = out.astype(bf16).reshape(n, chans, 4 * half)
+
+    def prepare_inverse(s):
+        got = recv[s].reshape(n * chans, 4 * half)
+        fbuf[...] = recv[s].astype(f32)
+        jbuf[...] = dot(got, perm[0]).reshape(n, chans, 4 * half)
+
+    def inverse(c):
+        pair = jnp.concatenate([fbuf[:, c, :], jbuf[:, c, :]], axis=0).astype(bf16)
+        lines = dot(txi[...], pair).astype(bf16)
+        return factor * dot(lines, tyi[...])
+
+    arrive(0)
+    spectrum = z_forward(0)
+    spec[...] = dot(spectrum, perm[3])
+    fold = dot(spectrum, perm[1])
+    gspec[...] = fold
+
+    def mixing(k, carry):
+        rows = pl.ds(pl.multiple_of(k * chans, chans), chans)
+        left_part = gspec[rows, :]
+        mix[rows, :] = jnp.sum(left_part[:, None, :] * wa[k].astype(f32), axis=0)
+        return carry
+
+    lax.fori_loop(0, modes, mixing, 0)
+    z_inverse(1)
+    ship(1)
+    arrive(1)
+    prepare_inverse(1)
+    for c in range(chans):
+        pre = inverse(c) + pwise[c] + bias_ref[c]
+        squared = pre * pre
+        tanh_val = jnp.tanh(SQRT_TWO_PI * pre * (1.0 + 0.044715 * squared))
+        slope = 0.5 * (1.0 + tanh_val) + (0.5 * SQRT_TWO_PI) * pre * (
+            1.0 - tanh_val * tanh_val
+        ) * (1.0 + 0.134145 * squared)
+        grad = (cot_ref[c].astype(f32) * slope).astype(bf16)
+        gp[c] = grad
+        bsum[pl.ds(c, 1), :] = jnp.sum(grad.astype(f32), axis=0, keepdims=True)
+    for c in range(chans):
+        forward(gp, c)
+
+    acc = jnp.zeros((chans * blk, chans * blk), f32)
+    for b in range(cx // blk):
+        rows = pl.ds(b * blk, blk)
+        acc += lax.dot_general(
+            x_ref[:, rows, :].reshape(chans * blk, cy),
+            gp[:, rows, :].reshape(chans * blk, cy),
+            kron_dims,
+            preferred_element_type=f32,
+        )
+    short = jnp.sum((acc * mask).reshape(chans, blk, chans * blk), axis=1)
+    lane_in = lax.broadcasted_iota(jnp.int32, (chans * blk, 4 * half), 0)
+    lane_out = lax.broadcasted_iota(jnp.int32, (chans * blk, 4 * half), 1)
+    gather = jnp.where(lane_in // blk == lane_out, 1.0, 0.0).astype(bf16)
+
+    def split(value):
+        high = value.astype(bf16)
+        rest = value - high.astype(f32)
+        mid = rest.astype(bf16)
+        low = (rest - mid.astype(f32)).astype(bf16)
+        return high, mid, low
+
+    sums = sum(dot(piece, gather) for piece in split(short))
+    bias_sum = jnp.sum(bsum[...], axis=1, keepdims=True)
+    lanes = lax.broadcasted_iota(jnp.int32, (chans, 4 * half), 1)
+    terms = factor * jnp.where(lanes == chans, bias_sum, sums)
+    step = chans + 1
+    block = jnp.zeros((chans, 4 * half), f32)
+    for place, piece in enumerate(split(terms)):
+        block += pltpu.roll(piece.astype(f32), 2 * half + place * step, 1)
+    send[2] = (fbuf[...] + block[None]).astype(bf16)
+    ship(2)
+    pointwise(gp, kron(False))
+    arrive(2)
+    grad_spectrum = z_forward(2)
+    gspec[...] = dot(grad_spectrum, perm[2])
+
+    def back(k, carry):
+        rows = pl.ds(pl.multiple_of(k * chans, chans), chans)
+        mix[rows, :] = jnp.sum(gspec[rows, :][None] * wa[k].astype(f32), axis=1)
+        return carry
+
+    lax.fori_loop(0, modes, back, 0)
+    z_inverse(3)
+    ship(3)
+
+    total = jnp.sum(recv[2].astype(f32), axis=0)
+    joined = jnp.zeros_like(total)
+    for place in range(3):
+        joined += pltpu.roll(total, 2 * half - place * step, 1)
+    term_ref[...] = joined
+    gspec[...] = dot(grad_spectrum, perm[4])
+
+    def outer(k, carry):
+        rows = pl.ds(pl.multiple_of(k * chans, chans), chans)
+        scale = jnp.where(k == 0, 1.0, 2.0)
+        prod = (scale * spec[rows, :])[:, None, :] * gspec[rows, :][None]
+        prod = prod.reshape(chans * chans, 4 * half)
+        folded = prod + pltpu.roll(prod, 2 * half, 1)
+        start = k * (2 * chans * chans)
+        sg_ref[pl.ds(start, chans * chans, stride=2), :] = folded[:, :half]
+        sg_ref[pl.ds(start + 1, chans * chans, stride=2), :] = folded[:, half : 2 * half]
+        return carry
+
+    lax.fori_loop(0, modes, outer, 0)
+    arrive(3)
+    prepare_inverse(3)
+    for c in range(chans):
+        dx_ref[c] = (inverse(c) + pwise[c]).astype(bf16)
+    for s in range(4):
+        left(s)
+
+
+def fused(layer_input, cotangent, spec_weight, point_weight, bias_term):
+    chans, cx, cy = layer_input.shape[2:]
+    modes = spec_weight.shape[0]
+    half = 2 * modes
+    planes = lax.axis_size("mp")
+    factor = 1.0 / math.sqrt(cx * cy * planes)
+    kc = modes * chans
+    rows = modes * chans * chans * 2
+
+    def const(value):
+        return jnp.asarray(np.asarray(value, np.float32).astype(ml_dtypes.bfloat16))
+
+    cos_x, msin_x = np_table(cx, half, True)
+    cos_y, msin_y = np_table(cy, half, True)
+    cos_z, msin_z = np_table(planes, modes, False)
+    zero_y = np.zeros_like(cos_y)
+    eye = np.eye(chans)
+    ty1 = np.concatenate([cos_y, msin_y, zero_y, zero_y], 1)
+    ty2 = np.concatenate([-msin_y, cos_y, zero_y, zero_y], 1)
+    tyi = ty1.T
+    txf = np.concatenate([cos_x.T, msin_x.T], 1)
+    txi = np.concatenate([cos_x, -msin_x], 1)
+    kf = np.stack([np.kron(cos_z.T, eye), np.kron(msin_z.T, eye)])
+    ki = np.stack([np.kron(cos_z, eye), np.kron(msin_z, eye)])
+    perm = np.stack(
+        [
+            lane_map(half, [(1, -1), (0, 1), (0, 0), (0, 0)]),
+            lane_map(half, [(0, 1), (1, 1), (1, 1), (0, 1)]),
+            lane_map(half, [(0, 1), (1, 1), (1, -1), (0, -1)]),
+            lane_map(half, [(0, 1), (0, 1), (1, 1), (1, 1)]),
+            lane_map(half, [(0, 1), (1, 1), (1, 1), (0, -1)]),
+            lane_map(half, [(0, 1), (0, 1), (0, 0), (0, 0)]),
+            lane_map(half, [(0, 0), (0, 0), (0, -1), (0, 1)]),
+        ]
+    )
+    mask = jnp.asarray(np.kron(np.ones((chans, chans)), np.eye(16)).astype(np.float32))
+    vmem = pl.BlockSpec(memory_space=pltpu.VMEM)
+    f32, bf16 = jnp.float32, jnp.bfloat16
+    dx, sg, terms = pl.pallas_call(
+        functools.partial(fused_kernel, planes, chans, cx, cy, modes, factor),
+        out_shape=(
+            jax.ShapeDtypeStruct((chans, cx, cy), bf16),
+            jax.ShapeDtypeStruct((rows, half), f32),
+            jax.ShapeDtypeStruct((chans, 4 * half), f32),
+        ),
+        in_specs=[vmem] * 4 + [pl.BlockSpec(memory_space=pltpu.SMEM)] + [vmem] * 9,
+        out_specs=(vmem, vmem, vmem),
+        scratch_shapes=[
+            pltpu.VMEM((4, planes, chans, 4 * half), bf16),
+            pltpu.VMEM((4, planes, chans, 4 * half), bf16),
+            pltpu.VMEM((planes, chans, 4 * half), f32),
+            pltpu.VMEM((planes, chans, 4 * half), f32),
+            pltpu.VMEM((kc, 4 * half), f32),
+            pltpu.VMEM((kc, 4 * half), f32),
+            pltpu.VMEM((2 * chans * chans, half), f32),
+            pltpu.VMEM((modes, chans, chans, 4 * half), bf16),
+            pltpu.VMEM((kc, 4 * half), f32),
+            pltpu.VMEM((chans, cx, cy), f32),
+            pltpu.VMEM((chans, cx, cy), bf16),
+            pltpu.VMEM((chans, cy), f32),
+            pltpu.SemaphoreType.DMA((4,)),
+            pltpu.SemaphoreType.DMA((4,)),
+        ],
+        compiler_params=pltpu.CompilerParams(
+            collective_id=0, has_side_effects=True, vmem_limit_bytes=48 * 1024 * 1024
+        ),
+    )(
+        layer_input.reshape(chans, cx, cy), cotangent.reshape(chans, cx, cy),
+        spec_weight.reshape(rows, half), point_weight, bias_term,
+        const(ty1), const(ty2), const(tyi), const(txf), const(txi), const(kf), const(ki),
+        const(perm), mask,
+    )
+    return (
+        dx.reshape(layer_input.shape),
+        sg.reshape(spec_weight.shape),
+        terms[:, :chans],
+        terms[:, chans],
+    )
+
+
 def shards(layer_input, cotangent, spec_weight, point_weight, bias_term):
     local_z, cells_x, cells_y = (layer_input.shape[1], layer_input.shape[3], layer_input.shape[4])
     depth_z = local_z * lax.axis_size("mp")
+    channels, half = (layer_input.shape[2], 2 * spec_weight.shape[0])
+    one_row = spec_weight.shape[4] == half and lax.axis_size("mp") == half
+    if (
+        layer_input.shape[0] == 1 and local_z == 1 and lax.axis_size("dp") == 1
+        and one_row and channels == 16 and half == 32 and cells_x == cells_y == 128
+    ):
+        return fused(layer_input, cotangent, spec_weight, point_weight, bias_term)
     mode_count = spec_weight.shape[0]
     table_x = dft_table(cells_x, 2 * mode_count, True)
     table_y = dft_table(cells_y, 2 * mode_count, True)

time: 79.3 us -> 62.3 us (0.79)
  Pallas kernels: 0 us -> 39.2 us
  starting transfers between devices: 16.8 us -> 0 us
  waiting for transfers between devices: 16.5 us -> 0 us
  other arithmetic: 15.3 us -> 0 us
  matrix products: 7.95 us -> 0 us
    pallas_call x0 -> x1, Pallas kernels: none -> 39.2 us  [fused(): pl.pallas_call(functools.partial(fused_kernel, planes, chans, cx, cy, mod...]
    all_to_all x4 -> x0, starting transfers between devices: 16.8 us -> none  [the longest x2 10.1 us: to_spectrum(): lax.all_to_all(planes, 'mp', split_axis=4, concat_axis=1, tiled=True)]
    all_to_all x4 -> x0, waiting for transfers between devices: 16.5 us -> none  [the longest x2 9.33 us: to_spectrum(): lax.all_to_all(planes, 'mp', split_axis=4, concat_axis=1, tiled=True)]
    unnamed x30 -> x31, local copies, waits for them, and re-layouts: 9.28 us -> 20.9 us
    dot_general x13 -> x0, matrix products: 7.95 us -> none  [mixed_dot(): jnp.einsum(formula, first_op, second_op, preferred_element_type=jnp.float32)]
    unnamed x2 -> x0, other arithmetic: 6.38 us -> none
    convert_element_type x4 -> x0, other arithmetic: 6.09 us -> none  [the longest x1 6 us: shards(): spec_grad = lax.psum(weight_terms(spectrum, grad_spectrum, mode_scale).as...]
    slice x4 -> x1, local copies, waits for them, and re-layouts: 5.36 us -> 0.69 us  [fused(): terms[:, chans]]
  transfers between devices with their start and end apart: 4 -> 0, of which waited for: 3 -> 0; matrix products, arithmetic and copies ran while one was open for 18% -> 0% of each run, Pallas kernels for 0% -> 0%
where the time goes in v2:
time: 62.3 us; the launch traced here: 61.5 us
  Pallas kernels  39.2 us (63%)
  local copies, waits for them, and re-layouts  21.6 us (35%)
  between operations  0.66 us (1%)
    pallas_call x1, Pallas kernels, fused(): pl.pallas_call(functools.partial(fused_kernel, planes, chans, cx, cy, mod...  39.2 us
    unnamed x31, local copies, waits for them, and re-layouts  20.9 us

profile of v2, /device:TPU:0, one launch (start us, length us, event | category | flops | bytes accessed | tf_op | source)
XLA Modules:
  0.0 61.5 jit_solution(220280490020742641)
XLA Ops:
  0.6 0.0 copy-start
  0.6 1.6 %copy-done = bf16[16,16,16,2,32]{4,3,2,1,0:T(2,128)(2,1)S(1)} copy-done((bf16[16,16,16,2,32]{4,3,2,1,0:T(2,128)(2,1)S(1)}, bf16[16,16,16,2,32]{4,3,2,1,0:T(2,128)(2,1)}, u32[]{:S(2)}) %copy-start) | copy-done | bytes 524312
  2.2 0.0 copy-start.1
  2.2 1.0 %copy-done.1 = bf16[1,1,16,128,128]{4,3,2,1,0:T(8,128)(2,1)S(1)} copy-done((bf16[1,1,16,128,128]{4,3,2,1,0:T(8,128)(2,1)S(1)}, bf16[1,1,16,128,128]{4,3,2,1,0:T(8,128)(2,1)}, u32[]{:S(2)}) %copy-start.1) | copy-done | bytes 524312
  3.3 0.0 copy-start.2
  3.3 1.0 %copy-done.2 = bf16[1,1,16,128,128]{4,3,2,1,0:T(8,128)(2,1)S(1)} copy-done((bf16[1,1,16,128,128]{4,3,2,1,0:T(8,128)(2,1)S(1)}, bf16[1,1,16,128,128]{4,3,2,1,0:T(8,128)(2,1)}, u32[]{:S(2)}) %copy-start.2) | copy-done | bytes 524312
  4.3 0.0 copy-start.3
  4.3 1.0 %copy-done.3 = bf16[2,512,256]{2,1,0:T(8,128)(2,1)S(1)} copy-done((bf16[2,512,256]{2,1,0:T(8,128)(2,1)S(1)}, bf16[2,512,256]{2,1,0:T(8,128)(2,1)}, u32[]{:S(2)}) %copy-start.3) | copy-done | bytes 524312
  5.4 0.0 copy-start.4
  5.4 1.0 %copy-done.4 = bf16[2,256,512]{2,1,0:T(8,128)(2,1)S(1)} copy-done((bf16[2,256,512]{2,1,0:T(8,128)(2,1)S(1)}, bf16[2,256,512]{2,1,0:T(8,128)(2,1)}, u32[]{:S(2)}) %copy-start.4) | copy-done | bytes 524312
  6.4 0.0 copy-start.5
  6.4 0.9 %copy-done.5 = f32[256,256]{1,0:T(8,128)S(1)} copy-done((f32[256,256]{1,0:T(8,128)S(1)}, f32[256,256]{1,0:T(8,128)}, u32[]{:S(2)}) %copy-start.5) | copy-done | bytes 262168
  7.3 0.0 copy-start.6
  7.3 0.9 %copy-done.6 = bf16[7,128,128]{2,1,0:T(8,128)(2,1)S(1)} copy-done((bf16[7,128,128]{2,1,0:T(8,128)(2,1)S(1)}, bf16[7,128,128]{2,1,0:T(8,128)(2,1)}, u32[]{:S(2)}) %copy-start.6) | copy-done | bytes 229400
  8.3 0.0 copy-start.7
  8.3 0.8 %copy-done.7 = bf16[128,64]{1,0:T(8,128)(2,1)S(1)} copy-done((bf16[128,64]{1,0:T(8,128)(2,1)S(1)}, bf16[128,64]{1,0:T(8,128)(2,1)}, u32[]{:S(2)}) %copy-start.7) | copy-done | bytes 16408
  9.0 0.0 copy-start.8
  9.0 0.8 %copy-done.8 = bf16[128,128]{1,0:T(8,128)(2,1)S(1)} copy-done((bf16[128,128]{1,0:T(8,128)(2,1)S(1)}, bf16[128,128]{1,0:T(8,128)(2,1)}, u32[]{:S(2)}) %copy-start.8) | copy-done | bytes 32792
  9.8 0.0 copy-start.9
  9.8 0.8 %copy-done.9 = bf16[128,128]{1,0:T(8,128)(2,1)S(1)} copy-done((bf16[128,128]{1,0:T(8,128)(2,1)S(1)}, bf16[128,128]{1,0:T(8,128)(2,1)}, u32[]{:S(2)}) %copy-start.9) | copy-done | bytes 32792
  10.6 0.0 copy-start.10
  10.6 0.8 %copy-done.10 = bf16[128,128]{1,0:T(8,128)(2,1)S(1)} copy-done((bf16[128,128]{1,0:T(8,128)(2,1)S(1)}, bf16[128,128]{1,0:T(8,128)(2,1)}, u32[]{:S(2)}) %copy-start.10) | copy-done | bytes 32792
  11.3 0.0 copy-start.11
  11.3 0.7 %copy-done.11 = bf16[32,256]{1,0:T(8,128)(2,1)S(1)} copy-done((bf16[32,256]{1,0:T(8,128)(2,1)S(1)}, bf16[32,256]{1,0:T(8,128)(2,1)}, u32[]{:S(2)}) %copy-start.11) | copy-done | bytes 16408
  12.0 0.0 copy-start.12
  12.0 0.7 %copy-done.12 = bf16[16,16]{1,0:T(8,128)(2,1)S(1)} copy-done((bf16[16,16]{1,0:T(8,128)(2,1)S(1)}, bf16[16,16]{1,0:T(8,128)(2,1)}, u32[]{:S(2)}) %copy-start.12) | copy-done | bytes 536
  12.7 0.0 copy-start.13
  12.7 0.7 %copy-done.13 = f32[16]{0:T(128)S(1)} copy-done((f32[16]{0:T(128)S(1)}, f32[16]{0:T(128)}, u32[]{:S(2)}) %copy-start.13) | copy-done | bytes 88
  13.4 39.2 %shard_map.165 = (bf16[16,128,128]{2,1,0:T(8,128)(2,1)S(1)}, f32[8192,32]{1,0:T(8,128)}, f32[16,128]{1,0:T(8,128)S(1)}) custom-call(bf16[16,128,128]{2,1,0:T(8,128)(2,1)S(1)} %bitcast.7, bf16[16,128,128]{2,1,0:T(8,128)(2,1)S(1)} %bitcast.8, bf16[8192,32]{1,0:T(8,128)(2,1)S(1)} %bitcast.6, bf16[16,16]{1,0:T(8,128)(2,1)S(1)} %copy-done.12, f32[16]{0:T(128)S(1)} %copy-done.13, ...), custom_call_target="tpu_custom_call" | custom-call | tf_op jit(solution)/shard_map/pallas_call | solution.py:429
  52.6 0.7 %slice_reduce_fusion = f32[16]{0:T(128)} fusion(f32[16,128]{1,0:T(8,128)S(1)} %get-tuple-element.9), kind=kLoop, calls=%fused_computation | loop fusion | bytes 128 | tf_op jit(solution)/shard_map/slice | solution.py:467
  53.3 0.8 %copy.21 = bf16[1,1,16,128,128]{4,3,2,1,0:T(8,128)(2,1)} copy(bf16[1,1,16,128,128]{4,3,2,1,0:T(8,128)(2,1)S(1)} %bitcast.9) | data formatting | bytes 1048576
  54.1 6.8 %copy.22 = f32[16,16,16,2,32]{4,3,2,1,0:T(2,128)} copy(f32[16,16,16,2,32]{4,3,2,1,0:T(2,128)} %bitcast.11) | data formatting | bytes 2097152
  60.9 0.6 copy.23
Async XLA Ops:
  0.6 1.6 %copy-start = (bf16[16,16,16,2,32]{4,3,2,1,0:T(2,128)(2,1)S(1)}, bf16[16,16,16,2,32]{4,3,2,1,0:T(2,128)(2,1)}, u32[]{:S(2)}) copy-start(bf16[16,16,16,2,32]{4,3,2,1,0:T(2,128)(2,1)} %param.16) | copy-start | bytes 1572868
  2.2 1.0 %copy-start.1 = (bf16[1,1,16,128,128]{4,3,2,1,0:T(8,128)(2,1)S(1)}, bf16[1,1,16,128,128]{4,3,2,1,0:T(8,128)(2,1)}, u32[]{:S(2)}) copy-start(bf16[1,1,16,128,128]{4,3,2,1,0:T(8,128)(2,1)} %param.14) | copy-start | bytes 1572868
  3.3 1.0 %copy-start.2 = (bf16[1,1,16,128,128]{4,3,2,1,0:T(8,128)(2,1)S(1)}, bf16[1,1,16,128,128]{4,3,2,1,0:T(8,128)(2,1)}, u32[]{:S(2)}) copy-start(bf16[1,1,16,128,128]{4,3,2,1,0:T(8,128)(2,1)} %param.15) | copy-start | bytes 1572868
  4.3 1.0 %copy-start.3 = (bf16[2,512,256]{2,1,0:T(8,128)(2,1)S(1)}, bf16[2,512,256]{2,1,0:T(8,128)(2,1)}, u32[]{:S(2)}) copy-start(bf16[2,512,256]{2,1,0:T(8,128)(2,1)} %constant.25.clone.ki) | copy-start | bytes 1572868
  5.4 1.0 %copy-start.4 = (bf16[2,256,512]{2,1,0:T(8,128)(2,1)S(1)}, bf16[2,256,512]{2,1,0:T(8,128)(2,1)}, u32[]{:S(2)}) copy-start(bf16[2,256,512]{2,1,0:T(8,128)(2,1)} %constant.24.clone.kf) | copy-start | bytes 1572868
  6.4 0.9 %copy-start.5 = (f32[256,256]{1,0:T(8,128)S(1)}, f32[256,256]{1,0:T(8,128)}, u32[]{:S(2)}) copy-start(f32[256,256]{1,0:T(8,128)} %constant.18.clone.mask_ref) | copy-start | bytes 786436
  7.3 0.9 %copy-start.6 = (bf16[7,128,128]{2,1,0:T(8,128)(2,1)S(1)}, bf16[7,128,128]{2,1,0:T(8,128)(2,1)}, u32[]{:S(2)}) copy-start(bf16[7,128,128]{2,1,0:T(8,128)(2,1)} %constant.26.clone.perm) | copy-start | bytes 688132
  8.3 0.8 %copy-start.7 = (bf16[128,64]{1,0:T(8,128)(2,1)S(1)}, bf16[128,64]{1,0:T(8,128)(2,1)}, u32[]{:S(2)}) copy-start(bf16[128,64]{1,0:T(8,128)(2,1)} %constant.23.clone.txi) | copy-start | bytes 49156
  9.0 0.8 %copy-start.8 = (bf16[128,128]{1,0:T(8,128)(2,1)S(1)}, bf16[128,128]{1,0:T(8,128)(2,1)}, u32[]{:S(2)}) copy-start(bf16[128,128]{1,0:T(8,128)(2,1)} %constant.21.clone.tyi) | copy-start | bytes 98308
  9.8 0.8 %copy-start.9 = (bf16[128,128]{1,0:T(8,128)(2,1)S(1)}, bf16[128,128]{1,0:T(8,128)(2,1)}, u32[]{:S(2)}) copy-start(bf16[128,128]{1,0:T(8,128)(2,1)} %constant.20.clone.ty2) | copy-start | bytes 98308
  10.6 0.8 %copy-start.10 = (bf16[128,128]{1,0:T(8,128)(2,1)S(1)}, bf16[128,128]{1,0:T(8,128)(2,1)}, u32[]{:S(2)}) copy-start(bf16[128,128]{1,0:T(8,128)(2,1)} %constant.19.clone.ty1) | copy-start | bytes 98308
  11.3 0.7 %copy-start.11 = (bf16[32,256]{1,0:T(8,128)(2,1)S(1)}, bf16[32,256]{1,0:T(8,128)(2,1)}, u32[]{:S(2)}) copy-start(bf16[32,256]{1,0:T(8,128)(2,1)} %constant.22.clone.txf) | copy-start | bytes 49156
  12.0 0.7 %copy-start.12 = (bf16[16,16]{1,0:T(8,128)(2,1)S(1)}, bf16[16,16]{1,0:T(8,128)(2,1)}, u32[]{:S(2)}) copy-start(bf16[16,16]{1,0:T(8,128)(2,1)} %pw_ref.1) | copy-start | bytes 1540
  12.7 0.7 %copy-start.13 = (f32[16]{0:T(128)S(1)}, f32[16]{0:T(128)}, u32[]{:S(2)}) copy-start(f32[16]{0:T(128)} %bias_ref.1) | copy-start | bytes 196

commit v3 on v2

--- a/solution.py
+++ b/solution.py
@@ -162,12 +162,25 @@
 
 def fused_kernel(
     planes, chans, cx, cy, modes, factor,
-    x_ref, cot_ref, w_ref, pw_ref, bias_ref,
-    ty1, ty2, tyi, txf, txi, kf, ki, perm, mask_ref,
-    dx_ref, sg_ref, term_ref,
-    send, recv, fbuf, jbuf, spec, gspec, wraw, wa, mix, pwise, gp, bsum,
-    send_sem, recv_sem,
+    x_hbm, cot_hbm, w_hbm, pw_hbm, bias_ref, *rest,
 ):
+    tables_hbm, (dx_ref, spec, gout, term_ref), rest = rest[:9], rest[9:13], rest[13:]
+    (send, recv, fbuf, jbuf, gspec, wraw, wa, mix, pwise, gp, bsum,
+     send_sem, recv_sem, load_sem, x_ref, cot_ref, w_ref, pw_ref) = rest[:18]
+    ty1, ty2, tyi, txf, txi, kf, ki, perm, mask_ref = rest[18:]
+    loads = [
+        pltpu.make_async_copy(source, target, load_sem.at[place])
+        for place, (source, target) in enumerate(
+            zip(
+                (x_hbm, *(tables_hbm[t] for t in (0, 1, 3, 7, 8, 5)), w_hbm, pw_hbm,
+                 cot_hbm, *(tables_hbm[t] for t in (2, 4, 6))),
+                (x_ref, ty1, ty2, txf, perm, mask_ref, kf, w_ref, pw_ref,
+                 cot_ref, tyi, txi, ki),
+            )
+        )
+    ]
+    for load in loads:
+        load.start()
     f32, bf16 = jnp.float32, jnp.bfloat16
     me = lax.axis_index("mp")
     n = planes
@@ -220,11 +233,16 @@
         )
         fbuf[:, c, :] = dot(txf[...], stacked)
 
+    for load in loads[:4]:
+        load.wait()
     for c in range(chans):
         forward(x_ref, c)
     send[0] = fbuf[...].astype(bf16)
     pl.semaphore_wait(barrier, n - 1)
     ship(0)
+
+    for load in loads[4:]:
+        load.wait()
 
     def spread(k, carry):
         rows = chans * chans
@@ -361,31 +379,39 @@
     z_inverse(3)
     ship(3)
 
-    total = jnp.sum(recv[2].astype(f32), axis=0)
-    joined = jnp.zeros_like(total)
-    for place in range(3):
-        joined += pltpu.roll(total, 2 * half - place * step, 1)
-    term_ref[...] = joined
-    gspec[...] = dot(grad_spectrum, perm[4])
-
-    def outer(k, carry):
-        rows = pl.ds(pl.multiple_of(k * chans, chans), chans)
-        scale = jnp.where(k == 0, 1.0, 2.0)
-        prod = (scale * spec[rows, :])[:, None, :] * gspec[rows, :][None]
-        prod = prod.reshape(chans * chans, 4 * half)
-        folded = prod + pltpu.roll(prod, 2 * half, 1)
-        start = k * (2 * chans * chans)
-        sg_ref[pl.ds(start, chans * chans, stride=2), :] = folded[:, :half]
-        sg_ref[pl.ds(start + 1, chans * chans, stride=2), :] = folded[:, half : 2 * half]
-        return carry
-
-    lax.fori_loop(0, modes, outer, 0)
+    term_ref[...] = jnp.sum(recv[2].astype(f32), axis=0)
+    gout[...] = dot(grad_spectrum, perm[4])
     arrive(3)
     prepare_inverse(3)
     for c in range(chans):
         dx_ref[c] = (inverse(c) + pwise[c]).astype(bf16)
     for s in range(4):
         left(s)
+
+
+def outer_kernel(modes, chans, spec, gspec, term_ref, sg_ref, point_ref, bias_ref):
+    half = 2 * modes
+    k = pl.program_id(0)
+
+    @pl.when(k == 0)
+    def _():
+        total = term_ref[...]
+        joined = jnp.zeros_like(total)
+        for place in range(3):
+            joined += pltpu.roll(total, 2 * half - place * (chans + 1), 1)
+        point_ref[...] = joined[:, :chans]
+        row = lax.broadcasted_iota(jnp.int32, (chans, chans), 0)
+        col = lax.broadcasted_iota(jnp.int32, (chans, chans), 1)
+        bias_ref[...] = jnp.sum(
+            jnp.where(row == col, joined[:, chans : chans + 1], 0.0), axis=0, keepdims=True
+        )
+
+    scale = jnp.where(k == 0, 1.0, 2.0)
+    prod = (scale * spec[...])[:, None, :] * gspec[...][None]
+    prod = prod.reshape(chans * chans, 4 * half)
+    folded = prod + pltpu.roll(prod, 2 * half, 1)
+    sg_ref[pl.ds(0, chans * chans, stride=2), :] = folded[:, :half]
+    sg_ref[pl.ds(1, chans * chans, stride=2), :] = folded[:, half : 2 * half]
 
 
 def fused(layer_input, cotangent, spec_weight, point_weight, bias_term):
@@ -424,23 +450,26 @@
         ]
     )
     mask = jnp.asarray(np.kron(np.ones((chans, chans)), np.eye(16)).astype(np.float32))
+    tables = [const(t) for t in (ty1, ty2, tyi, txf, txi, kf, ki, perm)] + [mask]
     vmem = pl.BlockSpec(memory_space=pltpu.VMEM)
+    hbm = pl.BlockSpec(memory_space=pltpu.HBM)
+    smem = pl.BlockSpec(memory_space=pltpu.SMEM)
     f32, bf16 = jnp.float32, jnp.bfloat16
-    dx, sg, terms = pl.pallas_call(
+    dx, spec, gspec, terms = pl.pallas_call(
         functools.partial(fused_kernel, planes, chans, cx, cy, modes, factor),
         out_shape=(
             jax.ShapeDtypeStruct((chans, cx, cy), bf16),
-            jax.ShapeDtypeStruct((rows, half), f32),
+            jax.ShapeDtypeStruct((kc, 4 * half), f32),
+            jax.ShapeDtypeStruct((kc, 4 * half), f32),
             jax.ShapeDtypeStruct((chans, 4 * half), f32),
         ),
-        in_specs=[vmem] * 4 + [pl.BlockSpec(memory_space=pltpu.SMEM)] + [vmem] * 9,
-        out_specs=(vmem, vmem, vmem),
+        in_specs=[hbm] * 4 + [smem] + [hbm] * 9,
+        out_specs=(vmem, vmem, vmem, vmem),
         scratch_shapes=[
             pltpu.VMEM((4, planes, chans, 4 * half), bf16),
             pltpu.VMEM((4, planes, chans, 4 * half), bf16),
             pltpu.VMEM((planes, chans, 4 * half), f32),
             pltpu.VMEM((planes, chans, 4 * half), f32),
-            pltpu.VMEM((kc, 4 * half), f32),
             pltpu.VMEM((kc, 4 * half), f32),
             pltpu.VMEM((2 * chans * chans, half), f32),
             pltpu.VMEM((modes, chans, chans, 4 * half), bf16),
@@ -450,21 +479,41 @@
             pltpu.VMEM((chans, cy), f32),
             pltpu.SemaphoreType.DMA((4,)),
             pltpu.SemaphoreType.DMA((4,)),
-        ],
+            pltpu.SemaphoreType.DMA((13,)),
+            pltpu.VMEM((chans, cx, cy), bf16),
+            pltpu.VMEM((chans, cx, cy), bf16),
+            pltpu.VMEM((rows, half), bf16),
+            pltpu.VMEM((chans, chans), bf16),
+        ]
+        + [pltpu.VMEM(t.shape, t.dtype) for t in tables],
         compiler_params=pltpu.CompilerParams(
-            collective_id=0, has_side_effects=True, vmem_limit_bytes=48 * 1024 * 1024
+            collective_id=0, has_side_effects=True, vmem_limit_bytes=60 * 1024 * 1024
         ),
     )(
         layer_input.reshape(chans, cx, cy), cotangent.reshape(chans, cx, cy),
-        spec_weight.reshape(rows, half), point_weight, bias_term,
-        const(ty1), const(ty2), const(tyi), const(txf), const(txi), const(kf), const(ki),
-        const(perm), mask,
-    )
+        spec_weight.reshape(rows, half), point_weight, bias_term, *tables,
+    )
+    lines = pl.BlockSpec((chans, 4 * half), lambda k: (k, 0))
+    sg, point, bias = pl.pallas_call(
+        functools.partial(outer_kernel, modes, chans),
+        grid=(modes,),
+        out_shape=(
+            jax.ShapeDtypeStruct((rows, half), f32),
+            jax.ShapeDtypeStruct((chans, chans), f32),
+            jax.ShapeDtypeStruct((1, chans), f32),
+        ),
+        in_specs=[lines, lines, pl.BlockSpec((chans, 4 * half), lambda k: (0, 0))],
+        out_specs=(
+            pl.BlockSpec((rows // modes, half), lambda k: (k, 0)),
+            pl.BlockSpec((chans, chans), lambda k: (0, 0)),
+            pl.BlockSpec((1, chans), lambda k: (0, 0)),
+        ),
+    )(spec, gspec, terms)
     return (
         dx.reshape(layer_input.shape),
         sg.reshape(spec_weight.shape),
-        terms[:, :chans],
-        terms[:, chans],
+        point,
+        bias.reshape(chans),
     )
 
 

time: 62.3 us -> 51.6 us (0.83)
  local copies, waits for them, and re-layouts: 21.6 us -> 1.88 us
  Pallas kernels: 39.2 us -> 48.2 us
    unnamed x31 -> x1, local copies, waits for them, and re-layouts: 20.9 us -> 1.88 us
    pallas_call x0 -> x1, Pallas kernels: none -> 9.84 us  [fused(): pl.pallas_call(functools.partial(outer_kernel, modes, chans), grid=(modes...]
    pallas_call x1, Pallas kernels: 39.2 us -> 38.4 us  [fused(): pl.pallas_call(functools.partial(fused_kernel, planes, chans, cx, cy, mod...]
    slice x1 -> x0, local copies, waits for them, and re-layouts: 0.69 us -> none  [fused(): terms[:, chans]]
where the time goes in v3:
time: 51.6 us; the launch traced here: 50.7 us
  Pallas kernels  48.2 us (93%)
  local copies, waits for them, and re-layouts  1.88 us (4%)
  between operations  0.64 us (1%)
    pallas_call x1, Pallas kernels, fused(): pl.pallas_call(functools.partial(fused_kernel, planes, chans, cx, cy, mod...  38.4 us
    pallas_call x1, Pallas kernels, fused(): pl.pallas_call(functools.partial(outer_kernel, modes, chans), grid=(modes...  9.84 us
    unnamed x1, local copies, waits for them, and re-layouts  1.88 us

profile of v3, /device:TPU:0, one launch (start us, length us, event | category | flops | bytes accessed | tf_op | source)
XLA Modules:
  0.0 50.7 jit_solution(17094128061709163645)
XLA Ops:
  0.6 38.4 %shard_map.165 = (bf16[16,128,128]{2,1,0:T(8,128)(2,1)}, f32[256,128]{1,0:T(8,128)}, f32[256,128]{1,0:T(8,128)}, f32[16,128]{1,0:T(8,128)}) custom-call(bf16[16,128,128]{2,1,0:T(8,128)(2,1)} %bitcast.7, bf16[16,128,128]{2,1,0:T(8,128)(2,1)} %bitcast.8, bf16[8192,32]{1,0:T(8,128)(2,1)} %bitcast.6, bf16[16,16]{1,0:T(8,128)(2,1)} %pw_hbm.1, f32[16]{0:T(128)} %bias_ref.1, ...), custom_call_target="tpu_custom_call" | custom-call | tf_op jit(solution)/shard_map/pallas_call | solution.py:458
  39.0 9.8 %shard_map.166 = (f32[8192,32]{1,0:T(8,128)}, f32[16,16]{1,0:T(8,128)}, f32[1,16]{1,0:T(1,128)}) custom-call(f32[256,128]{1,0:T(8,128)} %get-tuple-element.12.spec, f32[256,128]{1,0:T(8,128)} %get-tuple-element.13.gspec, f32[16,128]{1,0:T(8,128)} %get-tuple-element.14.term_ref), custom_call_target="tpu_custom_call" | custom-call | tf_op jit(solution)/shard_map/pallas_call | solution.py:497
  48.9 1.9 %copy.19 = bf16[1,1,16,128,128]{4,3,2,1,0:T(8,128)(2,1)} copy(bf16[1,1,16,128,128]{4,3,2,1,0:T(8,128)(2,1)} %bitcast.9) | data formatting | bytes 1048576

commit v4 on v3

--- a/solution.py
+++ b/solution.py
@@ -166,8 +166,9 @@
 ):
     tables_hbm, (dx_ref, spec, gout, term_ref), rest = rest[:9], rest[9:13], rest[13:]
     (send, recv, fbuf, jbuf, gspec, wraw, wa, mix, pwise, gp, bsum,
-     send_sem, recv_sem, load_sem, x_ref, cot_ref, w_ref, pw_ref) = rest[:18]
-    ty1, ty2, tyi, txf, txi, kf, ki, perm, mask_ref = rest[18:]
+     send_sem, recv_sem, load_sem, x_ref, cot_ref, w_ref, pw_ref,
+     tsend, trecv) = rest[:20]
+    ty1, ty2, tyi, txf, txi, kf, ki, perm, mask_ref = rest[20:]
     loads = [
         pltpu.make_async_copy(source, target, load_sem.at[place])
         for place, (source, target) in enumerate(
@@ -187,6 +188,7 @@
     half = 2 * modes
     kc = modes * chans
     blk = 16
+    pair_rows = chans // 2
 
     def dot(a, b):
         return jnp.dot(a, b, preferred_element_type=f32)
@@ -218,6 +220,22 @@
         lax.fori_loop(1, n, go, 0)
         recv[s, me] = send[s, me]
 
+    def spread_terms():
+        def go(j, carry):
+            other = lax.rem(me + j, n)
+            pltpu.make_async_remote_copy(
+                src_ref=tsend,
+                dst_ref=trecv.at[me],
+                send_sem=send_sem.at[4],
+                recv_sem=recv_sem.at[4],
+                device_id={"mp": other},
+                device_id_type=pl.DeviceIdType.MESH,
+            ).start()
+            return carry
+
+        lax.fori_loop(1, n, go, 0)
+        trecv[me] = tsend[...]
+
     def arrive(s):
         part = recv.at[s, pl.ds(0, n - 1)]
         pltpu.make_async_copy(part, part, recv_sem.at[s]).wait()
@@ -227,7 +245,7 @@
         pltpu.make_async_copy(part, part, send_sem.at[s]).wait()
 
     def forward(src_ref, c):
-        plane = src_ref[c]
+        plane = jnp.concatenate([src_ref[c], src_ref[c + pair_rows]], axis=1)
         stacked = jnp.concatenate(
             [dot(plane, ty1[...]).astype(bf16), dot(plane, ty2[...]).astype(bf16)], axis=0
         )
@@ -235,7 +253,7 @@
 
     for load in loads[:4]:
         load.wait()
-    for c in range(chans):
+    for c in range(pair_rows):
         forward(x_ref, c)
     send[0] = fbuf[...].astype(bf16)
     pl.semaphore_wait(barrier, n - 1)
@@ -280,7 +298,7 @@
     pointwise(x_ref, kron(True))
 
     def z_forward(s):
-        got = recv[s].reshape(n * chans, 4 * half)
+        got = recv[s].astype(f32).reshape(n * pair_rows, 4 * half).astype(bf16)
         turned = dot(got, perm[0]).astype(bf16)
         return (factor * (dot(kf[0], got) + dot(kf[1], turned))).astype(bf16)
 
@@ -289,26 +307,37 @@
         scale = jnp.where(
             lax.broadcasted_iota(jnp.int32, (kc, 4 * half), 0) < chans, 1.0, 2.0
         )
-        modes_in = (scale * folded).astype(bf16)
+        folded = (scale * folded).reshape(modes, chans, 4 * half)
+        lane = lax.broadcasted_iota(jnp.int32, (modes, pair_rows, 4 * half), 2)
+        packed = jnp.where(lane < 2 * half, folded[:, :pair_rows], folded[:, pair_rows:])
+        modes_in = packed.reshape(modes * pair_rows, 4 * half).astype(bf16)
         turned = dot(modes_in, perm[0]).astype(bf16)
         out = dot(ki[0], modes_in) - dot(ki[1], turned)
-        send[s] = out.astype(bf16).reshape(n, chans, 4 * half)
+        send[s] = out.reshape(n, pair_rows, 4 * half).astype(bf16)
 
     def prepare_inverse(s):
-        got = recv[s].reshape(n * chans, 4 * half)
-        fbuf[...] = recv[s].astype(f32)
-        jbuf[...] = dot(got, perm[0]).reshape(n, chans, 4 * half)
+        wide = recv[s].astype(f32)
+        got = wide.reshape(n * pair_rows, 4 * half).astype(bf16)
+        fbuf[...] = wide
+        jbuf[...] = dot(got, perm[0]).reshape(n, pair_rows, 4 * half)
 
     def inverse(c):
         pair = jnp.concatenate([fbuf[:, c, :], jbuf[:, c, :]], axis=0).astype(bf16)
         lines = dot(txi[...], pair).astype(bf16)
-        return factor * dot(lines, tyi[...])
+        both = factor * dot(lines, tyi[...])
+        return ((c, both[:, :cy]), (c + pair_rows, both[:, cy:]))
+
+    def expand(values, which):
+        parts = [
+            dot(values, perm[which + 6 * h]).reshape(modes, pair_rows, 4 * half)
+            for h in range(2)
+        ]
+        return jnp.concatenate(parts, axis=1).reshape(kc, 4 * half)
 
     arrive(0)
     spectrum = z_forward(0)
-    spec[...] = dot(spectrum, perm[3])
-    fold = dot(spectrum, perm[1])
-    gspec[...] = fold
+    spec[...] = expand(spectrum, 3)
+    gspec[...] = expand(spectrum, 1)
 
     def mixing(k, carry):
         rows = pl.ds(pl.multiple_of(k * chans, chans), chans)
@@ -321,8 +350,8 @@
     ship(1)
     arrive(1)
     prepare_inverse(1)
-    for c in range(chans):
-        pre = inverse(c) + pwise[c] + bias_ref[c]
+    for c, spectral in (item for p in range(pair_rows) for item in inverse(p)):
+        pre = spectral + pwise[c] + bias_ref[c]
         squared = pre * pre
         tanh_val = jnp.tanh(SQRT_TWO_PI * pre * (1.0 + 0.044715 * squared))
         slope = 0.5 * (1.0 + tanh_val) + (0.5 * SQRT_TWO_PI) * pre * (
@@ -331,8 +360,11 @@
         grad = (cot_ref[c].astype(f32) * slope).astype(bf16)
         gp[c] = grad
         bsum[pl.ds(c, 1), :] = jnp.sum(grad.astype(f32), axis=0, keepdims=True)
-    for c in range(chans):
+    for c in range(pair_rows):
         forward(gp, c)
+    send[2] = fbuf[...].astype(bf16)
+    ship(2)
+    pointwise(gp, kron(False))
 
     acc = jnp.zeros((chans * blk, chans * blk), f32)
     for b in range(cx // blk):
@@ -359,16 +391,11 @@
     bias_sum = jnp.sum(bsum[...], axis=1, keepdims=True)
     lanes = lax.broadcasted_iota(jnp.int32, (chans, 4 * half), 1)
     terms = factor * jnp.where(lanes == chans, bias_sum, sums)
-    step = chans + 1
-    block = jnp.zeros((chans, 4 * half), f32)
-    for place, piece in enumerate(split(terms)):
-        block += pltpu.roll(piece.astype(f32), 2 * half + place * step, 1)
-    send[2] = (fbuf[...] + block[None]).astype(bf16)
-    ship(2)
-    pointwise(gp, kron(False))
+    tsend[...] = terms[:pair_rows] + pltpu.roll(terms[pair_rows:], half, 1)
+    spread_terms()
     arrive(2)
     grad_spectrum = z_forward(2)
-    gspec[...] = dot(grad_spectrum, perm[2])
+    gspec[...] = expand(grad_spectrum, 2)
 
     def back(k, carry):
         rows = pl.ds(pl.multiple_of(k * chans, chans), chans)
@@ -379,39 +406,53 @@
     z_inverse(3)
     ship(3)
 
-    term_ref[...] = jnp.sum(recv[2].astype(f32), axis=0)
-    gout[...] = dot(grad_spectrum, perm[4])
+    gout[...] = expand(grad_spectrum, 4)
+    every = trecv.at[pl.ds(0, n - 1)]
+    pltpu.make_async_copy(every, every, recv_sem.at[4]).wait()
+    term_ref[...] = jnp.sum(trecv[...], axis=0)
     arrive(3)
     prepare_inverse(3)
-    for c in range(chans):
-        dx_ref[c] = (inverse(c) + pwise[c]).astype(bf16)
+    for c, spectral in (item for p in range(pair_rows) for item in inverse(p)):
+        dx_ref[c] = (spectral + pwise[c]).astype(bf16)
     for s in range(4):
         left(s)
-
-
-def outer_kernel(modes, chans, spec, gspec, term_ref, sg_ref, point_ref, bias_ref):
+    pltpu.make_async_copy(every, every, send_sem.at[4]).wait()
+
+
+def outer_kernel(modes, chans, spec, gspec, term_ref, sg_hbm, point_ref, bias_ref, sg_ref, sems):
     half = 2 * modes
-    k = pl.program_id(0)
-
-    @pl.when(k == 0)
-    def _():
-        total = term_ref[...]
-        joined = jnp.zeros_like(total)
-        for place in range(3):
-            joined += pltpu.roll(total, 2 * half - place * (chans + 1), 1)
-        point_ref[...] = joined[:, :chans]
-        row = lax.broadcasted_iota(jnp.int32, (chans, chans), 0)
-        col = lax.broadcasted_iota(jnp.int32, (chans, chans), 1)
-        bias_ref[...] = jnp.sum(
-            jnp.where(row == col, joined[:, chans : chans + 1], 0.0), axis=0, keepdims=True
-        )
-
-    scale = jnp.where(k == 0, 1.0, 2.0)
-    prod = (scale * spec[...])[:, None, :] * gspec[...][None]
-    prod = prod.reshape(chans * chans, 4 * half)
-    folded = prod + pltpu.roll(prod, 2 * half, 1)
-    sg_ref[pl.ds(0, chans * chans, stride=2), :] = folded[:, :half]
-    sg_ref[pl.ds(1, chans * chans, stride=2), :] = folded[:, half : 2 * half]
+    area = 2 * chans * chans
+
+    def put(k):
+        rows = pl.ds(pl.multiple_of(k * area, area), area)
+        return pltpu.make_async_copy(sg_ref.at[rows], sg_hbm.at[rows], sems.at[k])
+
+    def outer(k, carry):
+        rows = pl.ds(pl.multiple_of(k * chans, chans), chans)
+        scale = jnp.where(k == 0, 1.0, 2.0)
+        prod = (scale * spec[rows, :])[:, None, :] * gspec[rows, :][None]
+        prod = prod.reshape(chans * chans, 4 * half)
+        folded = prod + pltpu.roll(prod, 2 * half, 1)
+        sg_ref[pl.ds(k * area, chans * chans, stride=2), :] = folded[:, :half]
+        sg_ref[pl.ds(k * area + 1, chans * chans, stride=2), :] = folded[:, half : 2 * half]
+        put(k).start()
+        return carry
+
+    lax.fori_loop(0, modes, outer, 0)
+    total = term_ref[...]
+    joined = jnp.concatenate([total, pltpu.roll(total, 3 * half, 1)], axis=0)
+    point_ref[...] = joined[:, :chans]
+    row = lax.broadcasted_iota(jnp.int32, (chans, chans), 0)
+    col = lax.broadcasted_iota(jnp.int32, (chans, chans), 1)
+    bias_ref[...] = jnp.sum(
+        jnp.where(row == col, joined[:, chans : chans + 1], 0.0), axis=0, keepdims=True
+    )
+
+    def finish(k, carry):
+        put(k).wait()
+        return carry
+
+    lax.fori_loop(0, modes, finish, 0)
 
 
 def fused(layer_input, cotangent, spec_weight, point_weight, bias_term):
@@ -429,25 +470,29 @@
     cos_x, msin_x = np_table(cx, half, True)
     cos_y, msin_y = np_table(cy, half, True)
     cos_z, msin_z = np_table(planes, modes, False)
-    zero_y = np.zeros_like(cos_y)
-    eye = np.eye(chans)
-    ty1 = np.concatenate([cos_y, msin_y, zero_y, zero_y], 1)
-    ty2 = np.concatenate([-msin_y, cos_y, zero_y, zero_y], 1)
+    eye = np.eye(chans // 2)
+    two = np.eye(2)
+    ty1 = np.kron(two, np.concatenate([cos_y, msin_y], 1))
+    ty2 = np.kron(two, np.concatenate([-msin_y, cos_y], 1))
     tyi = ty1.T
     txf = np.concatenate([cos_x.T, msin_x.T], 1)
     txi = np.concatenate([cos_x, -msin_x], 1)
     kf = np.stack([np.kron(cos_z.T, eye), np.kron(msin_z.T, eye)])
     ki = np.stack([np.kron(cos_z, eye), np.kron(msin_z, eye)])
+    picks = (
+        [(0, 1), (1, 1), (1, 1), (0, 1)],
+        [(0, 1), (1, 1), (1, -1), (0, -1)],
+        [(0, 1), (0, 1), (1, 1), (1, 1)],
+        [(0, 1), (1, 1), (1, 1), (0, -1)],
+    )
     perm = np.stack(
-        [
-            lane_map(half, [(1, -1), (0, 1), (0, 0), (0, 0)]),
-            lane_map(half, [(0, 1), (1, 1), (1, 1), (0, 1)]),
-            lane_map(half, [(0, 1), (1, 1), (1, -1), (0, -1)]),
-            lane_map(half, [(0, 1), (0, 1), (1, 1), (1, 1)]),
-            lane_map(half, [(0, 1), (1, 1), (1, 1), (0, -1)]),
+        [lane_map(half, [(1, -1), (0, 1), (3, -1), (2, 1)])]
+        + [lane_map(half, pick) for pick in picks]
+        + [
             lane_map(half, [(0, 1), (0, 1), (0, 0), (0, 0)]),
             lane_map(half, [(0, 0), (0, 0), (0, -1), (0, 1)]),
         ]
+        + [lane_map(half, [(g + 2, sign) for g, sign in pick]) for pick in picks]
     )
     mask = jnp.asarray(np.kron(np.ones((chans, chans)), np.eye(16)).astype(np.float32))
     tables = [const(t) for t in (ty1, ty2, tyi, txf, txi, kf, ki, perm)] + [mask]
@@ -461,15 +506,15 @@
             jax.ShapeDtypeStruct((chans, cx, cy), bf16),
             jax.ShapeDtypeStruct((kc, 4 * half), f32),
             jax.ShapeDtypeStruct((kc, 4 * half), f32),
-            jax.ShapeDtypeStruct((chans, 4 * half), f32),
+            jax.ShapeDtypeStruct((chans // 2, 4 * half), f32),
         ),
         in_specs=[hbm] * 4 + [smem] + [hbm] * 9,
         out_specs=(vmem, vmem, vmem, vmem),
         scratch_shapes=[
-            pltpu.VMEM((4, planes, chans, 4 * half), bf16),
-            pltpu.VMEM((4, planes, chans, 4 * half), bf16),
-            pltpu.VMEM((planes, chans, 4 * half), f32),
-            pltpu.VMEM((planes, chans, 4 * half), f32),
+            pltpu.VMEM((4, planes, chans // 2, 4 * half), bf16),
+            pltpu.VMEM((4, planes, chans // 2, 4 * half), bf16),
+            pltpu.VMEM((planes, chans // 2, 4 * half), f32),
+            pltpu.VMEM((planes, chans // 2, 4 * half), f32),
             pltpu.VMEM((kc, 4 * half), f32),
             pltpu.VMEM((2 * chans * chans, half), f32),
             pltpu.VMEM((modes, chans, chans, 4 * half), bf16),
@@ -477,13 +522,15 @@
             pltpu.VMEM((chans, cx, cy), f32),
             pltpu.VMEM((chans, cx, cy), bf16),
             pltpu.VMEM((chans, cy), f32),
-            pltpu.SemaphoreType.DMA((4,)),
-            pltpu.SemaphoreType.DMA((4,)),
+            pltpu.SemaphoreType.DMA((5,)),
+            pltpu.SemaphoreType.DMA((5,)),
             pltpu.SemaphoreType.DMA((13,)),
             pltpu.VMEM((chans, cx, cy), bf16),
             pltpu.VMEM((chans, cx, cy), bf16),
             pltpu.VMEM((rows, half), bf16),
             pltpu.VMEM((chans, chans), bf16),
+            pltpu.VMEM((chans // 2, 4 * half), f32),
+            pltpu.VMEM((planes, chans // 2, 4 * half), f32),
         ]
         + [pltpu.VMEM(t.shape, t.dtype) for t in tables],
         compiler_params=pltpu.CompilerParams(
@@ -493,21 +540,17 @@
         layer_input.reshape(chans, cx, cy), cotangent.reshape(chans, cx, cy),
         spec_weight.reshape(rows, half), point_weight, bias_term, *tables,
     )
-    lines = pl.BlockSpec((chans, 4 * half), lambda k: (k, 0))
     sg, point, bias = pl.pallas_call(
         functools.partial(outer_kernel, modes, chans),
-        grid=(modes,),
         out_shape=(
             jax.ShapeDtypeStruct((rows, half), f32),
             jax.ShapeDtypeStruct((chans, chans), f32),
             jax.ShapeDtypeStruct((1, chans), f32),
         ),
-        in_specs=[lines, lines, pl.BlockSpec((chans, 4 * half), lambda k: (0, 0))],
-        out_specs=(
-            pl.BlockSpec((rows // modes, half), lambda k: (k, 0)),
-            pl.BlockSpec((chans, chans), lambda k: (0, 0)),
-            pl.BlockSpec((1, chans), lambda k: (0, 0)),
-        ),
+        in_specs=[vmem] * 3,
+        out_specs=(hbm, vmem, vmem),
+        scratch_shapes=[pltpu.VMEM((rows, half), f32), pltpu.SemaphoreType.DMA((modes,))],
+        compiler_params=pltpu.CompilerParams(vmem_limit_bytes=60 * 1024 * 1024),
     )(spec, gspec, terms)
     return (
         dx.reshape(layer_input.shape),

time: 51.6 us -> 42.1 us (0.82); the launches traced: 50.7 us -> 41.9 us
  Pallas kernels: 48.2 us -> 39.4 us
    pallas_call x1, Pallas kernels: 38.4 us -> 33.9 us  [fused(): pl.pallas_call(functools.partial(fused_kernel, planes, chans, cx, cy, mod...]
    pallas_call x1, Pallas kernels: 9.84 us -> 5.49 us  [fused(): pl.pallas_call(functools.partial(outer_kernel, modes, chans), out_shape=(...]
where the time goes in v4:
time: 42.1 us; the launch traced here: 41.9 us
  Pallas kernels  39.4 us (94%)
  local copies, waits for them, and re-layouts  1.89 us (4%)
  between operations  0.65 us (2%)
    pallas_call x1, Pallas kernels, fused(): pl.pallas_call(functools.partial(fused_kernel, planes, chans, cx, cy, mod...  33.9 us
    pallas_call x1, Pallas kernels, fused(): pl.pallas_call(functools.partial(outer_kernel, modes, chans), out_shape=(...  5.49 us
    unnamed x1, local copies, waits for them, and re-layouts  1.89 us

profile of v4, /device:TPU:0, one launch (start us, length us, event | category | flops | bytes accessed | tf_op | source)
XLA Modules:
  0.0 41.9 jit_solution(12170462896480903260)
XLA Ops:
  0.6 33.9 %shard_map.165 = (bf16[16,128,128]{2,1,0:T(8,128)(2,1)}, f32[256,128]{1,0:T(8,128)}, f32[256,128]{1,0:T(8,128)}, f32[8,128]{1,0:T(8,128)}) custom-call(bf16[16,128,128]{2,1,0:T(8,128)(2,1)} %bitcast.8, bf16[16,128,128]{2,1,0:T(8,128)(2,1)} %bitcast.9, bf16[8192,32]{1,0:T(8,128)(2,1)} %bitcast.6, bf16[16,16]{1,0:T(8,128)(2,1)} %pw_hbm.1, f32[16]{0:T(128)} %bias_ref.1, ...), custom_call_target="tpu_custom_call" | custom-call | tf_op jit(solution)/shard_map/pallas_call | solution.py:503
  34.5 5.5 %shard_map.166 = (f32[8192,32]{1,0:T(8,128)}, f32[16,16]{1,0:T(8,128)}, f32[1,16]{1,0:T(1,128)}) custom-call(f32[256,128]{1,0:T(8,128)} %get-tuple-element.12.spec, f32[256,128]{1,0:T(8,128)} %get-tuple-element.13.gspec, f32[8,128]{1,0:T(8,128)} %get-tuple-element.14.term_ref), custom_call_target="tpu_custom_call" | custom-call | tf_op jit(solution)/shard_map/pallas_call | solution.py:543
  40.0 1.9 %copy.19 = bf16[1,1,16,128,128]{4,3,2,1,0:T(8,128)(2,1)} copy(bf16[1,1,16,128,128]{4,3,2,1,0:T(8,128)(2,1)} %bitcast.7) | data formatting | bytes 1048576

commit v5 on v4

--- a/solution.py
+++ b/solution.py
@@ -164,7 +164,9 @@
     planes, chans, cx, cy, modes, factor,
     x_hbm, cot_hbm, w_hbm, pw_hbm, bias_ref, *rest,
 ):
-    tables_hbm, (dx_ref, spec, gout, term_ref), rest = rest[:9], rest[9:13], rest[13:]
+    tables_hbm, (got_ref, point_out, spec, gout, term_ref), rest = (
+        rest[:9], rest[9:14], rest[14:]
+    )
     (send, recv, fbuf, jbuf, gspec, wraw, wa, mix, pwise, gp, bsum,
      send_sem, recv_sem, load_sem, x_ref, cot_ref, w_ref, pw_ref,
      tsend, trecv) = rest[:20]
@@ -365,6 +367,8 @@
     send[2] = fbuf[...].astype(bf16)
     ship(2)
     pointwise(gp, kron(False))
+    handed = pltpu.make_async_copy(pwise, point_out, load_sem.at[13])
+    handed.start()
 
     acc = jnp.zeros((chans * blk, chans * blk), f32)
     for b in range(cx // blk):
@@ -410,16 +414,23 @@
     every = trecv.at[pl.ds(0, n - 1)]
     pltpu.make_async_copy(every, every, recv_sem.at[4]).wait()
     term_ref[...] = jnp.sum(trecv[...], axis=0)
+    handed.wait()
     arrive(3)
-    prepare_inverse(3)
-    for c, spectral in (item for p in range(pair_rows) for item in inverse(p)):
-        dx_ref[c] = (spectral + pwise[c]).astype(bf16)
+    got_ref[...] = recv[3]
     for s in range(4):
         left(s)
     pltpu.make_async_copy(every, every, send_sem.at[4]).wait()
 
 
-def outer_kernel(modes, chans, spec, gspec, term_ref, sg_hbm, point_ref, bias_ref, sg_ref, sems):
+def outer_kernel(
+    modes, chans, planes, factor,
+    spec, gspec, term_ref, got_ref, tyi, txi, turn, local_hbm,
+    dx_ref, sg_hbm, point_ref, bias_ref,
+    sg_ref, sems, local, fbuf, jbuf,
+):
+    f32, bf16 = jnp.float32, jnp.bfloat16
+    load = pltpu.make_async_copy(local_hbm, local, sems.at[modes])
+    load.start()
     half = 2 * modes
     area = 2 * chans * chans
 
@@ -447,6 +458,22 @@
     bias_ref[...] = jnp.sum(
         jnp.where(row == col, joined[:, chans : chans + 1], 0.0), axis=0, keepdims=True
     )
+
+    pair_rows = chans // 2
+    wide = got_ref[...].astype(f32)
+    flat = wide.reshape(planes * pair_rows, 4 * half).astype(bf16)
+    fbuf[...] = wide
+    jbuf[...] = jnp.dot(flat, turn[...], preferred_element_type=f32).reshape(
+        planes, pair_rows, 4 * half
+    )
+    load.wait()
+    cy = tyi.shape[1] // 2
+    for c in range(pair_rows):
+        pair = jnp.concatenate([fbuf[:, c, :], jbuf[:, c, :]], axis=0).astype(bf16)
+        rows_x = jnp.dot(txi[...], pair, preferred_element_type=f32).astype(bf16)
+        both = factor * jnp.dot(rows_x, tyi[...], preferred_element_type=f32)
+        dx_ref[c] = (both[:, :cy] + local[c]).astype(bf16)
+        dx_ref[c + pair_rows] = (both[:, cy:] + local[c + pair_rows]).astype(bf16)
 
     def finish(k, carry):
         put(k).wait()
@@ -500,16 +527,17 @@
     hbm = pl.BlockSpec(memory_space=pltpu.HBM)
     smem = pl.BlockSpec(memory_space=pltpu.SMEM)
     f32, bf16 = jnp.float32, jnp.bfloat16
-    dx, spec, gspec, terms = pl.pallas_call(
+    got, local, spec, gspec, terms = pl.pallas_call(
         functools.partial(fused_kernel, planes, chans, cx, cy, modes, factor),
         out_shape=(
-            jax.ShapeDtypeStruct((chans, cx, cy), bf16),
+            jax.ShapeDtypeStruct((planes, chans // 2, 4 * half), bf16),
+            jax.ShapeDtypeStruct((chans, cx, cy), f32),
             jax.ShapeDtypeStruct((kc, 4 * half), f32),
             jax.ShapeDtypeStruct((kc, 4 * half), f32),
             jax.ShapeDtypeStruct((chans // 2, 4 * half), f32),
         ),
         in_specs=[hbm] * 4 + [smem] + [hbm] * 9,
-        out_specs=(vmem, vmem, vmem, vmem),
+        out_specs=(vmem, hbm, vmem, vmem, vmem),
         scratch_shapes=[
             pltpu.VMEM((4, planes, chans // 2, 4 * half), bf16),
             pltpu.VMEM((4, planes, chans // 2, 4 * half), bf16),
@@ -524,7 +552,7 @@
             pltpu.VMEM((chans, cy), f32),
             pltpu.SemaphoreType.DMA((5,)),
             pltpu.SemaphoreType.DMA((5,)),
-            pltpu.SemaphoreType.DMA((13,)),
+            pltpu.SemaphoreType.DMA((14,)),
             pltpu.VMEM((chans, cx, cy), bf16),
             pltpu.VMEM((chans, cx, cy), bf16),
             pltpu.VMEM((rows, half), bf16),
@@ -540,18 +568,25 @@
         layer_input.reshape(chans, cx, cy), cotangent.reshape(chans, cx, cy),
         spec_weight.reshape(rows, half), point_weight, bias_term, *tables,
     )
-    sg, point, bias = pl.pallas_call(
-        functools.partial(outer_kernel, modes, chans),
+    dx, sg, point, bias = pl.pallas_call(
+        functools.partial(outer_kernel, modes, chans, planes, factor),
         out_shape=(
+            jax.ShapeDtypeStruct((chans, cx, cy), bf16),
             jax.ShapeDtypeStruct((rows, half), f32),
             jax.ShapeDtypeStruct((chans, chans), f32),
             jax.ShapeDtypeStruct((1, chans), f32),
         ),
-        in_specs=[vmem] * 3,
-        out_specs=(hbm, vmem, vmem),
-        scratch_shapes=[pltpu.VMEM((rows, half), f32), pltpu.SemaphoreType.DMA((modes,))],
+        in_specs=[vmem] * 7 + [hbm],
+        out_specs=(vmem, hbm, vmem, vmem),
+        scratch_shapes=[
+            pltpu.VMEM((rows, half), f32),
+            pltpu.SemaphoreType.DMA((modes + 1,)),
+            pltpu.VMEM((chans, cx, cy), f32),
+            pltpu.VMEM((planes, chans // 2, 4 * half), f32),
+            pltpu.VMEM((planes, chans // 2, 4 * half), f32),
+        ],
         compiler_params=pltpu.CompilerParams(vmem_limit_bytes=60 * 1024 * 1024),
-    )(spec, gspec, terms)
+    )(spec, gspec, terms, got, tables[2], tables[4], const(perm[0]), local)
     return (
         dx.reshape(layer_input.shape),
         sg.reshape(spec_weight.shape),

time: 42.1 us -> 39.6 us (0.941)
  local copies, waits for them, and re-layouts: 1.89 us -> 0 us
  Pallas kernels: 39.4 us -> 38.8 us
    unnamed x1 -> x0, local copies, waits for them, and re-layouts: 1.89 us -> none
    pallas_call x1, Pallas kernels: 33.9 us -> 32.6 us  [fused(): pl.pallas_call(functools.partial(fused_kernel, planes, chans, cx, cy, mod...]
    pallas_call x1, Pallas kernels: 5.49 us -> 6.19 us  [fused(): pl.pallas_call(functools.partial(outer_kernel, modes, chans, planes, fact...]
where the time goes in v5:
time: 39.6 us; the launch traced here: 39.5 us
  Pallas kernels  38.8 us (98%)
  between operations  0.64 us (2%)
    pallas_call x1, Pallas kernels, fused(): pl.pallas_call(functools.partial(fused_kernel, planes, chans, cx, cy, mod...  32.6 us
    pallas_call x1, Pallas kernels, fused(): pl.pallas_call(functools.partial(outer_kernel, modes, chans, planes, fact...  6.19 us

profile of v5, /device:TPU:0, one launch (start us, length us, event | category | flops | bytes accessed | tf_op | source)
XLA Modules:
  0.0 39.5 jit_solution(4278285729328594545)
XLA Ops:
  0.6 32.6 %shard_map.174 = (bf16[32,8,128]{2,1,0:T(8,128)(2,1)}, f32[16,128,128]{2,1,0:T(8,128)}, f32[256,128]{1,0:T(8,128)}, f32[256,128]{1,0:T(8,128)}, f32[8,128]{1,0:T(8,128)}) custom-call(bf16[16,128,128]{2,1,0:T(8,128)(2,1)} %bitcast.7, bf16[16,128,128]{2,1,0:T(8,128)(2,1)} %bitcast.8, bf16[8192,32]{1,0:T(8,128)(2,1)} %bitcast.6, bf16[16,16]{1,0:T(8,128)(2,1)} %pw_hbm.1, ...), custom_call_target="tpu_custom_call" | custom-call | tf_op jit(solution)/shard_map/pallas_call | solution.py:530
  33.3 6.2 %shard_map.175 = (bf16[16,128,128]{2,1,0:T(8,128)(2,1)}, f32[8192,32]{1,0:T(8,128)}, f32[16,16]{1,0:T(8,128)}, f32[1,16]{1,0:T(1,128)}) custom-call(f32[256,128]{1,0:T(8,128)} %get-tuple-element.13.spec, f32[256,128]{1,0:T(8,128)} %get-tuple-element.14.gspec, f32[8,128]{1,0:T(8,128)} %get-tuple-element.15.term_ref, ...), custom_call_target="tpu_custom_call" | custom-call | tf_op jit(solution)/shard_map/pallas_call | solution.py:571

commit v6 on v5

--- a/solution.py
+++ b/solution.py
@@ -338,7 +338,6 @@
 
     arrive(0)
     spectrum = z_forward(0)
-    spec[...] = expand(spectrum, 3)
     gspec[...] = expand(spectrum, 1)
 
     def mixing(k, carry):
@@ -347,9 +346,10 @@
         mix[rows, :] = jnp.sum(left_part[:, None, :] * wa[k].astype(f32), axis=0)
         return carry
 
-    lax.fori_loop(0, modes, mixing, 0)
+    lax.fori_loop(0, modes, mixing, 0, unroll=True)
     z_inverse(1)
     ship(1)
+    spec[...] = expand(spectrum, 3)
     arrive(1)
     prepare_inverse(1)
     for c, spectral in (item for p in range(pair_rows) for item in inverse(p)):
@@ -406,7 +406,7 @@
         mix[rows, :] = jnp.sum(gspec[rows, :][None] * wa[k].astype(f32), axis=1)
         return carry
 
-    lax.fori_loop(0, modes, back, 0)
+    lax.fori_loop(0, modes, back, 0, unroll=True)
     z_inverse(3)
     ship(3)
 
@@ -449,7 +449,7 @@
         put(k).start()
         return carry
 
-    lax.fori_loop(0, modes, outer, 0)
+    lax.fori_loop(0, modes, outer, 0, unroll=True)
     total = term_ref[...]
     joined = jnp.concatenate([total, pltpu.roll(total, 3 * half, 1)], axis=0)
     point_ref[...] = joined[:, :chans]

time: 39.6 us -> 37.8 us (0.955)
  Pallas kernels: 38.8 us -> 36.9 us
    pallas_call x1, Pallas kernels: 6.19 us -> 4.68 us  [fused(): pl.pallas_call(functools.partial(outer_kernel, modes, chans, planes, fact...]
where the time goes in v6:
time: 37.8 us; the launch traced here: 37.6 us
  Pallas kernels  36.9 us (98%)
  between operations  0.64 us (2%)
    pallas_call x1, Pallas kernels, fused(): pl.pallas_call(functools.partial(fused_kernel, planes, chans, cx, cy, mod...  32.3 us
    pallas_call x1, Pallas kernels, fused(): pl.pallas_call(functools.partial(outer_kernel, modes, chans, planes, fact...  4.68 us

profile of v6, /device:TPU:0, one launch (start us, length us, event | category | flops | bytes accessed | tf_op | source)
XLA Modules:
  0.0 37.6 jit_solution(7740049446945082714)
XLA Ops:
  0.6 32.3 %shard_map.174 = (bf16[32,8,128]{2,1,0:T(8,128)(2,1)}, f32[16,128,128]{2,1,0:T(8,128)}, f32[256,128]{1,0:T(8,128)}, f32[256,128]{1,0:T(8,128)}, f32[8,128]{1,0:T(8,128)}) custom-call(bf16[16,128,128]{2,1,0:T(8,128)(2,1)} %bitcast.7, bf16[16,128,128]{2,1,0:T(8,128)(2,1)} %bitcast.8, bf16[8192,32]{1,0:T(8,128)(2,1)} %bitcast.6, bf16[16,16]{1,0:T(8,128)(2,1)} %pw_hbm.1, ...), custom_call_target="tpu_custom_call" | custom-call | tf_op jit(solution)/shard_map/pallas_call | solution.py:530
  32.9 4.7 %shard_map.175 = (bf16[16,128,128]{2,1,0:T(8,128)(2,1)}, f32[8192,32]{1,0:T(8,128)}, f32[16,16]{1,0:T(8,128)}, f32[1,16]{1,0:T(1,128)}) custom-call(f32[256,128]{1,0:T(8,128)} %get-tuple-element.13.spec, f32[256,128]{1,0:T(8,128)} %get-tuple-element.14.gspec, f32[8,128]{1,0:T(8,128)} %get-tuple-element.15.term_ref, ...), custom_call_target="tpu_custom_call" | custom-call | tf_op jit(solution)/shard_map/pallas_call | solution.py:571
